TPU v7x, 512 devices: a whole 4x8x8 slice. The times are simulated.
512 devices in a mesh: freq: 16 (over x_hi, y), tx: 4 (over x_lo, core), ty: 8 (over z).
Axes of the slice: x: 4 (x_hi: 2, x_lo: 2; x = x_hi * 2 + x_lo), y: 8, z: 8, core: 2. Of those that a mesh axis runs over, the one named last changes fastest.
Arguments:
- wavefield: float32 [2, 32, 128, 2048], P(None, 'freq', 'tx', 'ty'), may hold values from -6 to 6
- coef_table: float32 [2, 32, 9, 32], P(None, 'freq'), may hold values from -2.4 to 2.4
- velocity_bins: int32 [4, 128, 2048], P(None, 'tx', 'ty'), may hold values from 0 to 30
- slab_fracs: float32 [32, 128, 2048], P('freq', 'tx', 'ty'), may hold values from 0 to 1
- owners: int32 [4], replicated, may hold values from 0 to 31
Outputs:
- wave_out: float32 [2, 32, 128, 2048], P(None, 'freq', 'tx', 'ty')
- images: float32 [4, 128, 2048], P(None, 'tx', 'ty')
All inputs are finite; a program needn't handle non-finite values.
Results may differ from a plain program's by a relative error of at most 0.0003.
Values sent between devices are 32-bit elements; how exact they have to be, the bound alone decides.
A program may use at most 64 MiB of HBM per device.

v0:
```python
import math

import jax
import jax.numpy as jnp
from jax import lax
from jax.sharding import PartitionSpec as P


def broadcast(x, axis, root):
    mine = lax.axis_index(axis) == root
    return lax.psum(jnp.where(mine, x, jnp.zeros_like(x)), axis)


def padded_2(x, sides, width):
    for axis, dim in sides:
        size, length = (lax.axis_size(axis), x.shape[dim])
        up = [(i, (i + 1) % size) for i in range(size - 1)]
        down = [(j, i) for i, j in up]
        last = lax.slice_in_dim(x, length - width, length, axis=dim)
        first = lax.slice_in_dim(x, 0, width, axis=dim)
        before = lax.ppermute(last, axis, up)
        after = lax.ppermute(first, axis, down)
        x = jnp.concatenate([before, x, after], axis=dim)
    return x


def smooth(padded):
    along_x = 0.25 * padded[:, :, :-2, :] + 0.5 * padded[:, :, 1:-1, :] + 0.25 * padded[:, :, 2:, :]
    along_y = (
        0.25 * along_x[:, :, :, :-2] + 0.5 * along_x[:, :, :, 1:-1] + 0.25 * along_x[:, :, :, 2:]
    )
    return 2.0 * along_y - padded[:, :, 1:-1, 1:-1]


def on_device(wavefield, coef_table, velocity_bins, slab_fracs, owners):
    freq_count = wavefield.shape[1]
    tile_rows = wavefield.shape[2]
    tile_cols = wavefield.shape[3]
    degree = coef_table.shape[2] - 1
    bin_count = coef_table.shape[3]
    depth_count = velocity_bins.shape[0]
    slabs_local = slab_fracs.shape[0]
    total_freqs = freq_count * lax.axis_size("freq")
    levels = jnp.arange(bin_count, dtype=jnp.int32)[:, None]
    wave_now = wavefield
    image_list = []
    for slice_index in range(depth_count):
        owner_slab = owners[slice_index]
        local_slab = lax.dynamic_index_in_dim(
            slab_fracs, owner_slab % slabs_local, 0, keepdims=False
        )
        fraction = broadcast(local_slab, "freq", owner_slab // slabs_local).reshape(-1)
        bin_index = velocity_bins[slice_index].reshape(-1)
        blending = jnp.where(
            levels == bin_index[None, :], 1.0 - fraction[None, :], jnp.float32(0.0)
        )
        blending = blending + jnp.where(
            levels == bin_index[None, :] + 1, fraction[None, :], jnp.float32(0.0)
        )

        def weighted(power, chebyshev):
            table_rows = coef_table[:, :, power, :].reshape(2 * freq_count, bin_count)
            coeff = jnp.dot(table_rows, blending, precision=lax.Precision.HIGHEST).reshape(
                2, freq_count, tile_rows, tile_cols
            )
            real_part = coeff[0] * chebyshev[0] - coeff[1] * chebyshev[1]
            imag_part = coeff[0] * chebyshev[1] + coeff[1] * chebyshev[0]
            return jnp.stack([real_part, imag_part])

        def operate(values):
            padded = padded_2(values, (("tx", 2), ("ty", 3)), 1)
            return smooth(padded)

        previous = wave_now
        current = operate(wave_now)
        summed = weighted(0, previous) + weighted(1, current)
        for power in range(2, degree + 1):
            following = 2.0 * operate(current) - previous
            summed = summed + weighted(power, following)
            previous, current = (current, following)
        wave_now = summed
        partial_image = jnp.sum(wave_now[0], axis=0) / math.sqrt(total_freqs)
        image_list.append(lax.psum(partial_image, "freq"))
    image_stack = jnp.stack(image_list)
    return (wave_now, image_stack)


def solution(mesh):
    in_specs = (
        P(None, "freq", "tx", "ty"),
        P(None, "freq", None, None),
        P(None, "tx", "ty"),
        P("freq", "tx", "ty"),
        P(),
    )
    out_specs = (P(None, "freq", "tx", "ty"), P(None, "tx", "ty"))
    return jax.shard_map(
        on_device, mesh=mesh, in_specs=in_specs, out_specs=out_specs, check_vma=False
    )
```

profile of v0, /device:TPU:64, one launch (start us, length us, event | category | flops | bytes accessed | tf_op | source)
XLA Modules:
  0.0 863.9 jit_solution(9527083580599787514)
XLA Ops:
  15.1 4.3 collective-permute-start.2
  22.3 3.8 collective-permute-done.3
  33.5 5.5 collective-permute-start.6
  41.0 5.5 collective-permute-done.7
  54.1 3.8 collective-permute-start.10
  60.4 3.8 collective-permute-done.11
  77.6 3.4 collective-permute-start.14
  83.9 3.4 collective-permute-done.15
  87.7 3.9 collective-permute-start.16
  93.6 3.8 collective-permute-done.17
  97.5 3.4 collective-permute-start.18
  114.6 3.4 collective-permute-start.22
  120.9 3.4 collective-permute-done.23
  124.7 3.2 collective-permute-start.24
  138.1 3.1 collective-permute-done.27
  141.6 3.6 collective-permute-start.28
  155.0 3.1 collective-permute-done.31
  158.5 107.4 %all-reduce.7.cloned.1.call-done = (f32[8192]{0:T(1024)}, f32[8192]{0:T(1024)}, f32[8192]{0:T(1024)}, f32[8192]{0:T(1024)}) async-done(((f32[8192]{0:T(1024)}, f32[8192]{0:T(1024)}, f32[8192]{0:T(1024)}, f32[8192]{0:T(1024)}), (f32[8192]{0:T(1024)}, f32[8192]{0:T(1024)}, f32[8192]{0:T(1024)}, f32[8192]{0:T(1024)})) %all-reduce.7.cloned.1.call-update) | async-done | bytes 131088 | tf_op jit(solution)/shard_map/psum | solution.py:11
  296.7 3.6 collective-permute-start.34
  303.4 3.1 collective-permute-done.35
  314.0 4.4 collective-permute-start.38
  321.2 4.7 collective-permute-done.39
  333.4 3.9 collective-permute-start.42
  340.1 3.5 collective-permute-done.43
  357.4 3.1 collective-permute-done.47
  374.3 3.1 collective-permute-done.51
  391.2 3.1 collective-permute-done.55
  408.0 3.1 collective-permute-done.59
  424.9 3.1 collective-permute-done.63
  509.5 3.1 collective-permute-done.83
  695.4 3.1 collective-permute-done.127
  699.8 155.5 %all-reduce.5.cloned.1.call-done = (f32[1,32,256]{2,1,0:T(8,128)}, f32[1,32,256]{2,1,0:T(8,128)}, f32[1,32,256]{2,1,0:T(8,128)}, f32[1,32,256]{2,1,0:T(8,128)}) async-done(((f32[1,32,256]{2,1,0:T(8,128)}, f32[1,32,256]{2,1,0:T(8,128)}, f32[1,32,256]{2,1,0:T(8,128)}, f32[1,32,256]{2,1,0:T(8,128)}), (f32[1,32,256]{2,1,0:T(8,128)}, f32[1,32,256]{2,1,0:T(8,128)}, f32[1,32,256]{2,1,0:T(8,128)}, ...) | async-done | bytes 131088 | tf_op jit(solution)/shard_map/psum | solution.py:83
  (578 shorter events, 462.8 us)
Async XLA Ops:
  7.2 258.8 %all-reduce.7.cloned.1.call-start = ((), (), s32[]{:S(2)}) async-start(), calls=%async_computation.1 | async-start | bytes 262144 | tf_op jit(solution)/shard_map/psum | solution.py:11
  15.1 7.2 collective-permute-start.2
  19.4 6.7 collective-permute-start.3
  33.5 7.5 collective-permute-start.6
  39.0 7.5 collective-permute-start.7
  47.0 7.0 collective-permute-start.8
  54.1 6.3 collective-permute-start.10
  57.9 6.3 collective-permute-start.11
  64.6 12.8 %collective-permute-start.12 = (f32[2,2,1,256]{3,2,1,0:T(1,128)S(1)}, f32[2,2,1,256]{3,2,1,0:T(1,128)S(1)}, u32[]{:S(2)}, u32[]{:S(2)}) collective-permute-start(f32[2,2,1,256]{3,2,1,0:T(1,128)S(1)} %get-tuple-element.261), channel_id=1, source_target_pairs={{0,8},{8,16},{16,24},{1,9},{9,17},{17,25},{2,10},{10,18},{18,26},{... | collective-permute-start | bytes 12296 | tf_op jit(solution)/shard_map/ppermute | solution.py:21
  67.5 10.0 %collective-permute-start.13 = (f32[2,2,1,256]{3,2,1,0:T(1,128)S(1)}, f32[2,2,1,256]{3,2,1,0:T(1,128)S(1)}, u32[]{:S(2)}, u32[]{:S(2)}) collective-permute-start(f32[2,2,1,256]{3,2,1,0:T(1,128)S(1)} %get-tuple-element.262), channel_id=1, source_target_pairs={{8,0},{16,8},{24,16},{9,1},{17,9},{25,17},{10,2},{18,10},{26,18},{... | collective-permute-start | bytes 12296 | tf_op jit(solution)/shard_map/ppermute | solution.py:22
  77.6 6.3 collective-permute-start.14
  81.0 6.3 collective-permute-start.15
  97.5 7.8 collective-permute-start.18
  100.8 6.3 collective-permute-start.19
  105.2 750.1 %all-reduce.5.cloned.1.call-start = ((), (), s32[]{:S(2)}) async-start(), calls=%async_computation | async-start | bytes 262144 | tf_op jit(solution)/shard_map/psum | solution.py:83
  114.6 6.3 collective-permute-start.22
  118.0 6.3 collective-permute-start.23
  131.7 6.3 collective-permute-start.26
  148.6 6.3 collective-permute-start.30
  151.8 6.3 collective-permute-start.31
  296.7 6.7 collective-permute-start.34
  300.2 6.3 collective-permute-start.35
  314.0 7.2 collective-permute-start.38
  318.4 7.5 collective-permute-start.39
  333.4 6.7 collective-permute-start.42
  435.6 6.9 collective-permute-start.66
  452.5 6.7 collective-permute-start.70
  469.4 6.7 collective-permute-start.74
  486.3 6.7 collective-permute-start.78
  570.9 6.7 collective-permute-start.98
  587.8 7.0 collective-permute-start.102
  604.7 6.5 collective-permute-start.106
  (108 other events, 524.5 us)
Sparse Core Ops, SparseCore 0:
  105.4 160.5 all-reduce.6
  699.9 155.3 all-reduce.4
where the time goes:
time: 872 us; the launch traced here: 864 us
  waiting for transfers between devices  452 us (52%)
  starting transfers between devices  323 us (37%)
  matrix products  31.8 us (4%)
  between operations  28.6 us (3%)
  other arithmetic  19.7 us (2%)
  local copies, waits for them, and re-layouts  9.35 us (1%)
    ppermute x64, starting transfers between devices, padded_2(): before = lax.ppermute(last, axis, up)  199 us
    ppermute x64, waiting for transfers between devices, padded_2(): after = lax.ppermute(first, axis, down)  179 us
    psum x1, waiting for transfers between devices, on_device(): image_list.append(lax.psum(partial_image, 'freq'))  156 us
    ppermute x64, starting transfers between devices, padded_2(): after = lax.ppermute(first, axis, down)  124 us
    psum x1, waiting for transfers between devices, broadcast(): return lax.psum(jnp.where(mine, x, jnp.zeros_like(x)), axis)  107 us
    dot_general x36, matrix products, weighted(): jnp.dot(table_rows, blending, precision=lax.Precision.HIGHEST)  31.8 us
  transfers between devices with their start and end apart: 130, of which 85 were waited for; matrix products, arithmetic and copies ran while one was open for 2% of the time, Pallas kernels for 0%

commit v1 on v0

v1 whole, which is shorter than its diff:
```python
import functools
import math

import jax
import jax.numpy as jnp
from jax import lax
from jax.experimental import pallas as pl
from jax.experimental.pallas import tpu as pltpu
from jax.sharding import PartitionSpec as P

MESH = pl.DeviceIdType.MESH
HALO = 8
LANES = 128
GROUP = 32


def kernel(
    sizes,
    owners,
    wave,
    table,
    bins,
    slabs,
    wave_out,
    images,
    wv,
    lnd,
    pk_l,
    pk_r,
    in_r,
    in_l,
    ext3,
    mask,
    tk,
    tab_a,
    tab_d,
    co_a,
    co_d,
    src1,
    src3,
    land1,
    land3,
    dst1,
    dst3,
    halo_send,
    halo_recv,
    rs_send,
    rs_recv,
    ag_send,
    ag_recv,
):
    n, n_tx, n_ty = sizes
    me, tx, ty = lax.axis_index("freq"), lax.axis_index("tx"), lax.axis_index("ty")
    _, freqs, rows, cols = wave.shape
    steps = bins.shape[0]
    orders = table.shape[2]
    row_tiles, col_tiles = rows // 8, cols // LANES
    tiles = row_tiles * col_tiles
    chunks = src1.shape[2]
    per = tiles // chunks
    fields = 2 * freqs
    mine, group = lax.rem(me, chunks), lax.div(me, chunks) * chunks

    up, down = lax.rem(tx + n_tx - 1, n_tx), lax.rem(tx + 1, n_tx)
    left, right = lax.rem(ty + n_ty - 1, n_ty), lax.rem(ty + 1, n_ty)

    def there(x, y):
        return {"tx": x, "ty": y}

    def peer(d):
        return lax.rem(me + d, n)

    barrier = pltpu.get_barrier_semaphore()
    for d in range(1, n):
        pl.semaphore_signal(barrier, inc=1, device_id={"freq": peer(d)}, device_id_type=MESH)
    for x in (up, tx, down):
        for y in (left, ty, right):
            if x is not tx or y is not ty:
                pl.semaphore_signal(barrier, inc=1, device_id=there(x, y), device_id_type=MESH)

    def parts(g):
        return (src1.at[g // 3], land1.at[g // 3], dst1.at[g // 3]) if g in (0, 3) else (src3.at[g - 1], land3.at[g - 1], dst3.at[g - 1])

    def scatter_copy(g, d):
        src, land, _ = parts(g)
        to = peer(d)
        return pltpu.make_async_remote_copy(
            src_ref=src.at[:, lax.rem(to, chunks)],
            dst_ref=land.at[d],
            send_sem=rs_send.at[g, d],
            recv_sem=rs_recv.at[g, d],
            device_id={"freq": to},
            device_id_type=MESH,
        )

    def gather_copy(g, d):
        _, _, dst = parts(g)
        return pltpu.make_async_remote_copy(
            src_ref=dst.at[:, mine],
            dst_ref=dst.at[:, mine],
            send_sem=ag_send.at[g, d],
            recv_sem=ag_recv.at[g, d],
            device_id={"freq": group + lax.rem(mine + d, chunks)},
            device_id_type=MESH,
        )

    def gather_wait(g, d):
        _, _, dst = parts(g)
        origin = lax.rem(mine + chunks - d, chunks)
        return pltpu.make_async_remote_copy(
            src_ref=dst.at[:, origin],
            dst_ref=dst.at[:, origin],
            send_sem=ag_send.at[g, d],
            recv_sem=ag_recv.at[g, d],
            device_id={"freq": group + origin},
            device_id_type=MESH,
        )

    def scatter(g):
        for d in range(1, n):
            scatter_copy(g, d).start()

    def reduce_and_gather(g):
        src, land, dst = parts(g)
        for d in range(1, n):
            scatter_copy(g, d).wait_recv()
        total = src[:, mine]
        for d in range(1, n):
            total = total + land[d]
        dst[:, mine] = total
        for d in range(1, chunks):
            gather_copy(g, d).start()

    def gathered(g):
        for d in range(1, chunks):
            gather_wait(g, d).wait_recv()

    def tile_at(r, c):
        t = r * col_tiles + c
        return t // per, pl.ds((t % per) * 8, 8)

    def halo_copies(s):
        pieces = [
            (wv.at[s, :, :, 0:HALO], lnd.at[s, :, :, 0:HALO], there(up, ty)),
            (wv.at[s, :, :, rows - HALO : rows], lnd.at[s, :, :, HALO : 2 * HALO], there(down, ty)),
            (pk_l.at[s], in_r.at[s, 0:rows], there(tx, left)),
            (pk_r.at[s], in_l.at[s, 0:rows], there(tx, right)),
            (pk_l.at[s, 0:HALO], in_r.at[s, rows : rows + HALO], there(up, left)),
            (pk_l.at[s, rows - HALO : rows], in_r.at[s, rows + HALO : rows + 2 * HALO], there(down, left)),
            (pk_r.at[s, 0:HALO], in_l.at[s, rows : rows + HALO], there(up, right)),
            (pk_r.at[s, rows - HALO : rows], in_l.at[s, rows + HALO : rows + 2 * HALO], there(down, right)),
        ]
        return [
            pltpu.make_async_remote_copy(
                src_ref=src,
                dst_ref=dst,
                send_sem=halo_send.at[s, i],
                recv_sem=halo_recv.at[s, i],
                device_id=to,
                device_id_type=MESH,
            )
            for i, (src, dst, to) in enumerate(pieces)
        ]

    lane = lax.broadcasted_iota(jnp.int32, (rows, LANES), 1)

    def pack(s):
        packed_l = packed_r = None
        for c in range(2):
            for f in range(freqs):
                at = (c * freqs + f) * GROUP
                first = wv[s, c, f, :, 0:LANES]
                last = wv[s, c, f, :, cols - LANES : cols]
                if at == 0:
                    packed_l, packed_r = first, last
                else:
                    packed_l = jnp.where(lane // GROUP == at // GROUP, pltpu.roll(first, at, 1), packed_l)
                    packed_r = jnp.where(lane // GROUP == at // GROUP - 1, pltpu.roll(last, at, 1), packed_r)
        pk_l[s] = packed_l
        pk_r[s] = packed_r

    def send_halos(s):
        pack(s)
        for copy in halo_copies(s):
            copy.start()

    for c in range(2):
        for f in range(freqs):
            wv[0, c, f] = wave[c, f]
    pack(0)
    per_slab = slabs.shape[0]
    for j in range(steps):
        owner = owners[j]
        src = src1.at[0, 0] if j == 0 else src3.at[0, j - 1]
        for r in range(row_tiles):
            for c in range(col_tiles):
                value = jnp.zeros((8, LANES), jnp.float32)
                for i in range(per_slab):
                    tile = slabs[i, 8 * r : 8 * r + 8, LANES * c : LANES * c + LANES]
                    value = jnp.where(jnp.full((8, LANES), owner) == me * per_slab + i, tile, value)
                chunk, at = tile_at(r, c)
                src[chunk, at] = value

    pl.semaphore_wait(barrier, n - 1 + 8)
    scatter(0)
    for copy in halo_copies(0):
        copy.start()
    scatter(1)

    tab_a[...] = jnp.zeros_like(tab_a)
    for c in range(2):
        for f in range(freqs):
            tab_a[c * freqs + f, 0:orders, 0 : table.shape[3]] = table[c, f]
    for i in range(fields):
        tab_d[i] = pltpu.roll(tab_a[i], LANES - 1, 1) - tab_a[i]

    ext_rows, ext_cols = rows + 2 * HALO, cols + LANES
    r = lax.broadcasted_iota(jnp.int32, (ext_rows, ext_cols), 0)
    c = lax.broadcasted_iota(jnp.int32, (ext_rows, ext_cols), 1)
    no_down = jnp.where(tx == n_tx - 1, 1, 0)
    no_up = jnp.where(tx == 0, 1, 0)
    no_right = jnp.where(ty == n_ty - 1, 1, 0)
    no_left = jnp.where(ty == 0, 1, 0)
    outside = jnp.where(r >= rows + HALO, no_up, jnp.where(r >= rows, no_down, 0))
    outside = outside + jnp.where(c >= cols + LANES // 2, no_left, jnp.where(c >= cols, no_right, 0))
    mask[...] = jnp.where(outside > 0, 0.0, 0.25)

    def lookup(s):
        def one(i, carry):
            for r in range(row_tiles):
                for c in range(col_tiles):
                    rs, cs = slice(8 * r, 8 * r + 8), slice(LANES * c, LANES * c + LANES)
                    index = bins[s, rs, cs]
                    for k in range(orders):
                        for tab, co in ((tab_a, co_a), (tab_d, co_d)):
                            row = jnp.broadcast_to(tab[i, k : k + 1, :], (8, LANES))
                            co[i, k, rs, cs] = jnp.take_along_axis(row, index, axis=1, mode="promise_in_bounds")
            return carry

        lax.fori_loop(0, fields, one, 0)

    def smooth(v):
        v = v + pltpu.roll(v, 1, 0)
        v = v + pltpu.roll(v, ext_rows - 1, 0)
        v = v + pltpu.roll(v, 1, 1)
        return v + pltpu.roll(v, ext_cols - 1, 1)

    ext_lane = lax.broadcasted_iota(jnp.int32, (ext_rows, LANES), 1)

    def recurrence(s):
        both = jnp.where(lax.rem(ext_lane, GROUP) < GROUP // 2, in_r[s], in_l[s])
        for i in range(fields):
            ext3[i] = both if i == 0 else pltpu.roll(both, LANES - i * GROUP, 1)

        def one(i, carry):
            c, f = i // freqs, lax.rem(i, freqs)
            quarter = mask[...]
            own = jnp.concatenate([wv[s, c, f], lnd[s, c, f]], axis=0)
            t = jnp.concatenate([own, ext3[i]], axis=1) * (4.0 * quarter)
            p = None
            for k in range(1, orders):
                w = smooth(t) * quarter
                p = 0.5 * w if k == 1 else w - p
                t = p - t
                tk[k - 1, i] = t[0:rows, 0:cols]
            return carry

        lax.fori_loop(0, fields, one, 0)

    scale = 1.0 / math.sqrt(freqs * n)

    def combine(s):
        frac = dst1.at[0, 0] if s == 0 else dst3.at[0, s - 1]
        image = src1.at[1, 0] if s == steps - 1 else src3.at[1, s]
        for r in range(row_tiles):
            for c in range(col_tiles):
                rs, cs = slice(8 * r, 8 * r + 8), slice(LANES * c, LANES * c + LANES)
                chunk, at = tile_at(r, c)
                fraction = frac[chunk, at]
                summed = None
                for f in range(freqs):
                    re = im = None
                    for k in range(orders):
                        t_re = wv[s, 0, f, rs, cs] if k == 0 else tk[k - 1, f, rs, cs]
                        t_im = wv[s, 1, f, rs, cs] if k == 0 else tk[k - 1, freqs + f, rs, cs]
                        c_re = co_a[f, k, rs, cs] + fraction * co_d[f, k, rs, cs]
                        c_im = co_a[freqs + f, k, rs, cs] + fraction * co_d[freqs + f, k, rs, cs]
                        add_re = c_re * t_re - c_im * t_im
                        add_im = c_re * t_im + c_im * t_re
                        re = add_re if k == 0 else re + add_re
                        im = add_im if k == 0 else im + add_im
                    if s == steps - 1:
                        wave_out[0, f, rs, cs] = re
                        wave_out[1, f, rs, cs] = im
                    else:
                        wv[s + 1, 0, f, rs, cs] = re
                        wv[s + 1, 1, f, rs, cs] = im
                    summed = re if f == 0 else summed + re
                image[chunk, at] = summed * scale

    lookup(0)
    reduce_and_gather(0)
    for s in range(steps):
        for copy in halo_copies(s):
            copy.wait_recv()
        recurrence(s)
        if s == 0:
            gathered(0)
        if s == 1:
            gathered(1)
        combine(s)
        if s < steps - 1:
            send_halos(s + 1)
            if s == 0:
                reduce_and_gather(1)
            if s == steps - 2:
                scatter(2)
            lookup(s + 1)

    scatter(3)
    reduce_and_gather(2)
    reduce_and_gather(3)

    def put_image(j, src):
        for r in range(row_tiles):
            for c in range(col_tiles):
                chunk, at = tile_at(r, c)
                images[j, 8 * r : 8 * r + 8, LANES * c : LANES * c + LANES] = src[chunk, at]

    gathered(2)
    for j in range(steps - 1):
        put_image(j, dst3.at[1, j])
    for s in range(steps):
        for copy in halo_copies(s):
            copy.wait_send()
    for g in range(4):
        for d in range(1, n):
            scatter_copy(g, d).wait_send()
        for d in range(1, chunks):
            if g < 3:
                gather_copy(g, d).wait_send()
    gathered(3)
    put_image(steps - 1, dst1.at[1, 0])
    for d in range(1, chunks):
        gather_copy(3, d).wait_send()


def solution(mesh):
    n, n_tx, n_ty = (mesh.shape[axis] for axis in ("freq", "tx", "ty"))

    def on_device(wavefield, coef_table, velocity_bins, slab_fracs, owners):
        _, freqs, rows, cols = wavefield.shape
        orders = coef_table.shape[2]
        steps = velocity_bins.shape[0]
        tiles = rows // 8 * (cols // LANES)
        chunks = min(n, tiles)
        chunk = (chunks, tiles // chunks * 8, LANES)
        fields = 2 * freqs
        ext_rows, ext_cols = rows + 2 * HALO, cols + LANES
        f32 = jnp.float32
        vmem = pl.BlockSpec(memory_space=pltpu.VMEM)
        dma = pltpu.SemaphoreType.DMA
        return pl.pallas_call(
            functools.partial(kernel, (n, n_tx, n_ty)),
            out_shape=(
                jax.ShapeDtypeStruct(wavefield.shape, f32),
                jax.ShapeDtypeStruct((steps, rows, cols), f32),
            ),
            in_specs=[pl.BlockSpec(memory_space=pltpu.SMEM)] + [vmem] * 4,
            out_specs=(vmem, vmem),
            scratch_shapes=[
                pltpu.VMEM((steps, 2, freqs, rows, cols), f32),
                pltpu.VMEM((steps, 2, freqs, 2 * HALO, cols), f32),
                pltpu.VMEM((steps, rows, LANES), f32),
                pltpu.VMEM((steps, rows, LANES), f32),
                pltpu.VMEM((steps, ext_rows, LANES), f32),
                pltpu.VMEM((steps, ext_rows, LANES), f32),
                pltpu.VMEM((fields, ext_rows, LANES), f32),
                pltpu.VMEM((ext_rows, ext_cols), f32),
                pltpu.VMEM((orders - 1, fields, rows, cols), f32),
                pltpu.VMEM((fields, 16, LANES), f32),
                pltpu.VMEM((fields, 16, LANES), f32),
                pltpu.VMEM((fields, orders, rows, cols), f32),
                pltpu.VMEM((fields, orders, rows, cols), f32),
                pltpu.VMEM((2, 1) + chunk, f32),
                pltpu.VMEM((2, steps - 1) + chunk, f32),
                pltpu.VMEM((2, n, 1) + chunk[1:], f32),
                pltpu.VMEM((2, n, steps - 1) + chunk[1:], f32),
                pltpu.VMEM((2, 1) + chunk, f32),
                pltpu.VMEM((2, steps - 1) + chunk, f32),
                dma((steps, 8)),
                dma((steps, 8)),
                dma((4, n)),
                dma((4, n)),
                dma((4, chunks)),
                dma((4, chunks)),
            ],
            compiler_params=pltpu.CompilerParams(
                collective_id=0, has_side_effects=True, vmem_limit_bytes=32 * 1024 * 1024
            ),
        )(owners, wavefield, coef_table, velocity_bins, slab_fracs)

    in_specs = (
        P(None, "freq", "tx", "ty"),
        P(None, "freq", None, None),
        P(None, "tx", "ty"),
        P("freq", "tx", "ty"),
        P(),
    )
    out_specs = (P(None, "freq", "tx", "ty"), P(None, "tx", "ty"))
    return jax.shard_map(on_device, mesh=mesh, in_specs=in_specs, out_specs=out_specs, check_vma=False)
```

time: 872 us -> 77.4 us (0.09)
  the two profiles are of different devices: /device:TPU:64 before, /device:TPU:1 now
where the time goes in v1:
time: 77.4 us; the launch traced here: 77.1 us
  Pallas kernels  71.8 us (93%)
  local copies, waits for them, and re-layouts  4.7 us (6%)
    pallas_call x1, Pallas kernels, on_device(): pl.pallas_call(functools.partial(kernel, (n, n_tx, n_ty)), out_shape=(jax...  71.8 us
    unnamed x11, local copies, waits for them, and re-layouts  4.7 us

profile of v1, /device:TPU:1, one launch (start us, length us, event | category | flops | bytes accessed | tf_op | source)
XLA Modules:
  0.0 77.1 jit_solution(15466774250100993934)
XLA Ops:
  0.6 0.0 copy-start.3
  0.6 0.7 copy.7.table
  1.4 0.0 copy-done.3
  1.4 0.0 copy-start
  1.4 0.9 %copy-done = f32[2,2,32,256]{3,2,1,0:T(8,128)S(1)} copy-done((f32[2,2,32,256]{3,2,1,0:T(8,128)S(1)}, f32[2,2,32,256]{3,2,1,0:T(8,128)}, u32[]{:S(2)}) %copy-start) | copy-done | bytes 131096
  2.3 0.0 copy-start.1
  2.3 0.9 %copy-done.1 = s32[4,32,256]{2,1,0:T(8,128)S(1)} copy-done((s32[4,32,256]{2,1,0:T(8,128)S(1)}, s32[4,32,256]{2,1,0:T(8,128)}, u32[]{:S(2)}) %copy-start.1) | copy-done | bytes 131096
  3.2 0.0 copy-start.2
  3.2 0.8 %copy-done.2 = f32[2,32,256]{2,1,0:T(8,128)S(1)} copy-done((f32[2,32,256]{2,1,0:T(8,128)S(1)}, f32[2,32,256]{2,1,0:T(8,128)}, u32[]{:S(2)}) %copy-start.2) | copy-done | bytes 65560
  4.0 71.8 %shard_map.68 = (f32[2,2,32,256]{3,2,1,0:T(8,128)S(1)}, f32[4,32,256]{2,1,0:T(8,128)S(1)}) custom-call(s32[4]{0:T(128)S(1)} %copy-done.3, f32[2,2,32,256]{3,2,1,0:T(8,128)S(1)} %copy-done, f32[2,2,9,32]{3,2,1,0:T(8,128)S(1)} %copy.7.table, s32[4,32,256]{2,1,0:T(8,128)S(1)} %copy-done.1, f32[2,32,256]{2,1,0:T(8,128)S(1)} %copy-done.2), custom_call_target="tpu_custom_call" | custom-call | tf_op jit(solution)/shard_map/pallas_call | solution.py:363
  75.8 0.7 copy.10
  76.4 0.7 copy.11
Async XLA Ops:
  0.6 0.7 copy-start.3
  1.4 0.9 %copy-start = (f32[2,2,32,256]{3,2,1,0:T(8,128)S(1)}, f32[2,2,32,256]{3,2,1,0:T(8,128)}, u32[]{:S(2)}) copy-start(f32[2,2,32,256]{3,2,1,0:T(8,128)} %wave.1) | copy-start | bytes 393220
  2.3 0.9 %copy-start.1 = (s32[4,32,256]{2,1,0:T(8,128)S(1)}, s32[4,32,256]{2,1,0:T(8,128)}, u32[]{:S(2)}) copy-start(s32[4,32,256]{2,1,0:T(8,128)} %bins.1) | copy-start | bytes 393220
  3.2 0.8 %copy-start.2 = (f32[2,32,256]{2,1,0:T(8,128)S(1)}, f32[2,32,256]{2,1,0:T(8,128)}, u32[]{:S(2)}) copy-start(f32[2,32,256]{2,1,0:T(8,128)} %slabs.1) | copy-start | bytes 196612

commit v2 on v1

--- a/solution.py
+++ b/solution.py
@@ -17,12 +17,14 @@
 def kernel(
     sizes,
     owners,
-    wave,
+    wave_hbm,
     table,
+    bins_hbm,
+    slabs_hbm,
+    wave_out,
+    images,
     bins,
     slabs,
-    wave_out,
-    images,
     wv,
     lnd,
     pk_l,
@@ -42,6 +44,7 @@
     land3,
     dst1,
     dst3,
+    in_sem,
     halo_send,
     halo_recv,
     rs_send,
@@ -51,9 +54,9 @@
 ):
     n, n_tx, n_ty = sizes
     me, tx, ty = lax.axis_index("freq"), lax.axis_index("tx"), lax.axis_index("ty")
-    _, freqs, rows, cols = wave.shape
+    _, freqs, rows, cols = wave_hbm.shape
     steps = bins.shape[0]
-    orders = table.shape[2]
+    orders = table.shape[1]
     row_tiles, col_tiles = rows // 8, cols // LANES
     tiles = row_tiles * col_tiles
     chunks = src1.shape[2]
@@ -69,6 +72,14 @@
 
     def peer(d):
         return lax.rem(me + d, n)
+
+    inputs = [
+        pltpu.make_async_copy(slabs_hbm, slabs, in_sem.at[0]),
+        pltpu.make_async_copy(wave_hbm, wv.at[0], in_sem.at[1]),
+        pltpu.make_async_copy(bins_hbm, bins, in_sem.at[2]),
+    ]
+    for copy in inputs:
+        copy.start()
 
     barrier = pltpu.get_barrier_semaphore()
     for d in range(1, n):
@@ -87,8 +98,8 @@
         return pltpu.make_async_remote_copy(
             src_ref=src.at[:, lax.rem(to, chunks)],
             dst_ref=land.at[d],
-            send_sem=rs_send.at[g, d],
-            recv_sem=rs_recv.at[g, d],
+            send_sem=rs_send.at[g],
+            recv_sem=rs_recv.at[g],
             device_id={"freq": to},
             device_id_type=MESH,
         )
@@ -98,23 +109,14 @@
         return pltpu.make_async_remote_copy(
             src_ref=dst.at[:, mine],
             dst_ref=dst.at[:, mine],
-            send_sem=ag_send.at[g, d],
-            recv_sem=ag_recv.at[g, d],
+            send_sem=ag_send.at[g],
+            recv_sem=ag_recv.at[g],
             device_id={"freq": group + lax.rem(mine + d, chunks)},
             device_id_type=MESH,
         )
 
-    def gather_wait(g, d):
-        _, _, dst = parts(g)
-        origin = lax.rem(mine + chunks - d, chunks)
-        return pltpu.make_async_remote_copy(
-            src_ref=dst.at[:, origin],
-            dst_ref=dst.at[:, origin],
-            send_sem=ag_send.at[g, d],
-            recv_sem=ag_recv.at[g, d],
-            device_id={"freq": group + origin},
-            device_id_type=MESH,
-        )
+    def wait_for(ref, sem):
+        pltpu.make_async_copy(ref, ref, sem).wait()
 
     def scatter(g):
         for d in range(1, n):
@@ -122,8 +124,7 @@
 
     def reduce_and_gather(g):
         src, land, dst = parts(g)
-        for d in range(1, n):
-            scatter_copy(g, d).wait_recv()
+        wait_for(land.at[1:n], rs_recv.at[g])
         total = src[:, mine]
         for d in range(1, n):
             total = total + land[d]
@@ -132,8 +133,7 @@
             gather_copy(g, d).start()
 
     def gathered(g):
-        for d in range(1, chunks):
-            gather_wait(g, d).wait_recv()
+        wait_for(parts(g)[2].at[:, 1:chunks], ag_recv.at[g])
 
     def tile_at(r, c):
         t = r * col_tiles + c
@@ -141,14 +141,14 @@
 
     def halo_copies(s):
         pieces = [
-            (wv.at[s, :, :, 0:HALO], lnd.at[s, :, :, 0:HALO], there(up, ty)),
-            (wv.at[s, :, :, rows - HALO : rows], lnd.at[s, :, :, HALO : 2 * HALO], there(down, ty)),
-            (pk_l.at[s], in_r.at[s, 0:rows], there(tx, left)),
-            (pk_r.at[s], in_l.at[s, 0:rows], there(tx, right)),
-            (pk_l.at[s, 0:HALO], in_r.at[s, rows : rows + HALO], there(up, left)),
-            (pk_l.at[s, rows - HALO : rows], in_r.at[s, rows + HALO : rows + 2 * HALO], there(down, left)),
-            (pk_r.at[s, 0:HALO], in_l.at[s, rows : rows + HALO], there(up, right)),
-            (pk_r.at[s, rows - HALO : rows], in_l.at[s, rows + HALO : rows + 2 * HALO], there(down, right)),
+            (0, wv.at[s, :, :, 0:HALO], lnd.at[s, :, :, 0:HALO], there(up, ty)),
+            (0, wv.at[s, :, :, rows - HALO : rows], lnd.at[s, :, :, HALO : 2 * HALO], there(down, ty)),
+            (1, pk_l.at[s], in_r.at[s, 0:rows], there(tx, left)),
+            (2, pk_r.at[s], in_l.at[s, 0:rows], there(tx, right)),
+            (1, pk_l.at[s, 0:HALO], in_r.at[s, rows : rows + HALO], there(up, left)),
+            (1, pk_l.at[s, rows - HALO : rows], in_r.at[s, rows + HALO : rows + 2 * HALO], there(down, left)),
+            (2, pk_r.at[s, 0:HALO], in_l.at[s, rows : rows + HALO], there(up, right)),
+            (2, pk_r.at[s, rows - HALO : rows], in_l.at[s, rows + HALO : rows + 2 * HALO], there(down, right)),
         ]
         return [
             pltpu.make_async_remote_copy(
@@ -159,8 +159,12 @@
                 device_id=to,
                 device_id_type=MESH,
             )
-            for i, (src, dst, to) in enumerate(pieces)
+            for i, src, dst, to in pieces
         ]
+
+    def halo_wait(s, sems):
+        for i, landing in enumerate((lnd, in_r, in_l)):
+            wait_for(landing.at[s], sems.at[s, i])
 
     lane = lax.broadcasted_iota(jnp.int32, (rows, LANES), 1)
 
@@ -184,10 +188,7 @@
         for copy in halo_copies(s):
             copy.start()
 
-    for c in range(2):
-        for f in range(freqs):
-            wv[0, c, f] = wave[c, f]
-    pack(0)
+    inputs[0].wait()
     per_slab = slabs.shape[0]
     for j in range(steps):
         owner = owners[j]
@@ -201,6 +202,8 @@
                 chunk, at = tile_at(r, c)
                 src[chunk, at] = value
 
+    inputs[1].wait()
+    pack(0)
     pl.semaphore_wait(barrier, n - 1 + 8)
     scatter(0)
     for copy in halo_copies(0):
@@ -210,7 +213,7 @@
     tab_a[...] = jnp.zeros_like(tab_a)
     for c in range(2):
         for f in range(freqs):
-            tab_a[c * freqs + f, 0:orders, 0 : table.shape[3]] = table[c, f]
+            tab_a[c * freqs + f, 0:orders, 0 : table.shape[3]] = table[c, :, f]
     for i in range(fields):
         tab_d[i] = pltpu.roll(tab_a[i], LANES - 1, 1) - tab_a[i]
 
@@ -239,12 +242,6 @@
 
         lax.fori_loop(0, fields, one, 0)
 
-    def smooth(v):
-        v = v + pltpu.roll(v, 1, 0)
-        v = v + pltpu.roll(v, ext_rows - 1, 0)
-        v = v + pltpu.roll(v, 1, 1)
-        return v + pltpu.roll(v, ext_cols - 1, 1)
-
     ext_lane = lax.broadcasted_iota(jnp.int32, (ext_rows, LANES), 1)
 
     def recurrence(s):
@@ -252,20 +249,24 @@
         for i in range(fields):
             ext3[i] = both if i == 0 else pltpu.roll(both, LANES - i * GROUP, 1)
 
-        def one(i, carry):
-            c, f = i // freqs, lax.rem(i, freqs)
-            quarter = mask[...]
+        for i in range(fields):
+            c, f = i // freqs, i % freqs
             own = jnp.concatenate([wv[s, c, f], lnd[s, c, f]], axis=0)
-            t = jnp.concatenate([own, ext3[i]], axis=1) * (4.0 * quarter)
-            p = None
-            for k in range(1, orders):
-                w = smooth(t) * quarter
-                p = 0.5 * w if k == 1 else w - p
-                t = p - t
-                tk[k - 1, i] = t[0:rows, 0:cols]
-            return carry
-
-        lax.fori_loop(0, fields, one, 0)
+            tk[0, i] = jnp.concatenate([own, ext3[i]], axis=1) * (4.0 * mask[...])
+        for k in range(1, orders):
+            twice, summed, moved = [], [], []
+            for i in range(fields):
+                t = tk[k - 1, i]
+                twice.append(t + t)
+                summed.append(twice[i] + (pltpu.roll(t, 1, 0) + pltpu.roll(t, ext_rows - 1, 0)))
+            for i in range(fields):
+                moved.append(pltpu.roll(summed[i], 1, 1) + pltpu.roll(summed[i], ext_cols - 1, 1))
+            for i in range(fields):
+                w = (summed[i] + summed[i] + moved[i]) * mask[...]
+                if k == 1:
+                    tk[k, i] = 0.5 * (w - twice[i])
+                else:
+                    tk[k, i] = (w - tk[k - 2, i]) - twice[i]
 
     scale = 1.0 / math.sqrt(freqs * n)
 
@@ -281,8 +282,8 @@
                 for f in range(freqs):
                     re = im = None
                     for k in range(orders):
-                        t_re = wv[s, 0, f, rs, cs] if k == 0 else tk[k - 1, f, rs, cs]
-                        t_im = wv[s, 1, f, rs, cs] if k == 0 else tk[k - 1, freqs + f, rs, cs]
+                        t_re = tk[k, f, rs, cs]
+                        t_im = tk[k, freqs + f, rs, cs]
                         c_re = co_a[f, k, rs, cs] + fraction * co_d[f, k, rs, cs]
                         c_im = co_a[freqs + f, k, rs, cs] + fraction * co_d[freqs + f, k, rs, cs]
                         add_re = c_re * t_re - c_im * t_im
@@ -298,11 +299,11 @@
                     summed = re if f == 0 else summed + re
                 image[chunk, at] = summed * scale
 
+    inputs[2].wait()
     lookup(0)
     reduce_and_gather(0)
     for s in range(steps):
-        for copy in halo_copies(s):
-            copy.wait_recv()
+        halo_wait(s, halo_recv)
         recurrence(s)
         if s == 0:
             gathered(0)
@@ -331,18 +332,14 @@
     for j in range(steps - 1):
         put_image(j, dst3.at[1, j])
     for s in range(steps):
-        for copy in halo_copies(s):
-            copy.wait_send()
+        halo_wait(s, halo_send)
     for g in range(4):
-        for d in range(1, n):
-            scatter_copy(g, d).wait_send()
-        for d in range(1, chunks):
-            if g < 3:
-                gather_copy(g, d).wait_send()
+        wait_for(parts(g)[1].at[1:n], rs_send.at[g])
+        if g < 3:
+            wait_for(parts(g)[2].at[:, 1:chunks], ag_send.at[g])
     gathered(3)
     put_image(steps - 1, dst1.at[1, 0])
-    for d in range(1, chunks):
-        gather_copy(3, d).wait_send()
+    wait_for(dst1.at[1, :, 1:chunks], ag_send.at[3])
 
 
 def solution(mesh):
@@ -359,6 +356,7 @@
         ext_rows, ext_cols = rows + 2 * HALO, cols + LANES
         f32 = jnp.float32
         vmem = pl.BlockSpec(memory_space=pltpu.VMEM)
+        hbm = pl.BlockSpec(memory_space=pltpu.HBM)
         dma = pltpu.SemaphoreType.DMA
         return pl.pallas_call(
             functools.partial(kernel, (n, n_tx, n_ty)),
@@ -366,9 +364,11 @@
                 jax.ShapeDtypeStruct(wavefield.shape, f32),
                 jax.ShapeDtypeStruct((steps, rows, cols), f32),
             ),
-            in_specs=[pl.BlockSpec(memory_space=pltpu.SMEM)] + [vmem] * 4,
+            in_specs=[pl.BlockSpec(memory_space=pltpu.SMEM), hbm, vmem, hbm, hbm],
             out_specs=(vmem, vmem),
             scratch_shapes=[
+                pltpu.VMEM(velocity_bins.shape, jnp.int32),
+                pltpu.VMEM(slab_fracs.shape, f32),
                 pltpu.VMEM((steps, 2, freqs, rows, cols), f32),
                 pltpu.VMEM((steps, 2, freqs, 2 * HALO, cols), f32),
                 pltpu.VMEM((steps, rows, LANES), f32),
@@ -377,7 +377,7 @@
                 pltpu.VMEM((steps, ext_rows, LANES), f32),
                 pltpu.VMEM((fields, ext_rows, LANES), f32),
                 pltpu.VMEM((ext_rows, ext_cols), f32),
-                pltpu.VMEM((orders - 1, fields, rows, cols), f32),
+                pltpu.VMEM((orders, fields, ext_rows, ext_cols), f32),
                 pltpu.VMEM((fields, 16, LANES), f32),
                 pltpu.VMEM((fields, 16, LANES), f32),
                 pltpu.VMEM((fields, orders, rows, cols), f32),
@@ -388,17 +388,18 @@
                 pltpu.VMEM((2, n, steps - 1) + chunk[1:], f32),
                 pltpu.VMEM((2, 1) + chunk, f32),
                 pltpu.VMEM((2, steps - 1) + chunk, f32),
-                dma((steps, 8)),
-                dma((steps, 8)),
-                dma((4, n)),
-                dma((4, n)),
-                dma((4, chunks)),
-                dma((4, chunks)),
+                dma((3,)),
+                dma((steps, 3)),
+                dma((steps, 3)),
+                dma((4,)),
+                dma((4,)),
+                dma((4,)),
+                dma((4,)),
             ],
             compiler_params=pltpu.CompilerParams(
-                collective_id=0, has_side_effects=True, vmem_limit_bytes=32 * 1024 * 1024
+                collective_id=0, has_side_effects=True, vmem_limit_bytes=60 * 1024 * 1024
             ),
-        )(owners, wavefield, coef_table, velocity_bins, slab_fracs)
+        )(owners, wavefield, jnp.transpose(coef_table, (0, 2, 1, 3)), velocity_bins, slab_fracs)
 
     in_specs = (
         P(None, "freq", "tx", "ty"),

time: 77.4 us -> 60.6 us (0.78)
  Pallas kernels: 71.8 us -> 57.5 us
  local copies, waits for them, and re-layouts: 4.7 us -> 2.26 us
    pallas_call x1, Pallas kernels: 71.8 us -> 57.5 us  [on_device(): pl.pallas_call(functools.partial(kernel, (n, n_tx, n_ty)), out_shape=(jax...]
    unnamed x11 -> x4, local copies, waits for them, and re-layouts: 4.7 us -> 2.26 us
where the time goes in v2:
time: 60.6 us; the launch traced here: 60.4 us
  Pallas kernels  57.5 us (95%)
  local copies, waits for them, and re-layouts  2.26 us (4%)
  between operations  0.65 us (1%)
    pallas_call x1, Pallas kernels, on_device(): pl.pallas_call(functools.partial(kernel, (n, n_tx, n_ty)), out_shape=(jax...  57.5 us
    unnamed x4, local copies, waits for them, and re-layouts  2.26 us

profile of v2, /device:TPU:1, one launch (start us, length us, event | category | flops | bytes accessed | tf_op | source)
XLA Modules:
  0.0 60.4 jit_solution(2698355439298997786)
XLA Ops:
  0.6 57.5 %shard_map.68 = (f32[2,2,32,256]{3,2,1,0:T(8,128)}, f32[4,32,256]{2,1,0:T(8,128)}) custom-call(s32[4]{0:T(128)} %owners.1, f32[2,2,32,256]{3,2,1,0:T(8,128)} %wave_hbm.1, f32[2,9,2,32]{3,2,1,0:T(2,128)} %bitcast.1, s32[4,32,256]{2,1,0:T(8,128)} %bins_hbm.1, f32[2,32,256]{2,1,0:T(8,128)} %slabs_hbm.1), custom_call_target="tpu_custom_call" | custom-call | tf_op jit(solution)/shard_map/pallas_call | solution.py:361
  58.1 0.0 copy-start
  58.1 1.6 %copy.9 = f32[2,2,32,256]{3,2,1,0:T(8,128)} copy(f32[2,2,32,256]{3,2,1,0:T(8,128)} %get-tuple-element.4) | data formatting | bytes 262144
  59.7 0.0 copy-done
  59.7 0.7 %copy.10 = f32[4,32,256]{2,1,0:T(8,128)} copy(f32[4,32,256]{2,1,0:T(8,128)S(1)} %copy-done) | data formatting | bytes 262144
Async XLA Ops:
  58.1 1.6 %copy-start = (f32[4,32,256]{2,1,0:T(8,128)S(1)}, f32[4,32,256]{2,1,0:T(8,128)}, u32[]{:S(2)}) copy-start(f32[4,32,256]{2,1,0:T(8,128)} %get-tuple-element.5) | copy-start | bytes 393220

commit v3 on v0

v3 whole, which is shorter than its diff:
```python
import functools
import math

import jax
import jax.numpy as jnp
from jax import lax
from jax.experimental import pallas as pl
from jax.experimental.pallas import tpu as pltpu
from jax.sharding import PartitionSpec as P

MESH = pl.DeviceIdType.MESH
LANES = 128
GROUP = 32
DEG = 8


def widths(steps):
    return [0] + [DEG * (steps - 1 - s) for s in range(1, steps)]


def kernel(sizes, outs, *refs):
    n, n_tx, n_ty = sizes
    refs = list(refs)

    def take(count):
        got = refs[:count]
        del refs[:count]
        return got

    owners, wave_hbm, table, bins_hbm, slabs_hbm, wave_out, images = take(7)
    bins, slabs = take(2)
    wv, lnd, pk_l, pk_r, in_r, in_l = (take(2) for _ in range(6))
    first, co_a, co_d = (take(len(outs)) for _ in range(3))
    tk, mask, tab_a, tab_d = take(4)
    bins_dn, bins_up, bins_r, bins_l, frac_dn, frac_up, frac_r, frac_l = take(8)
    src1, src3, land1, land3, dst1, dst3 = take(6)
    in_sem, halo_send, halo_recv, side_send, side_recv, rs_send, rs_recv, ag_send, ag_recv = take(9)

    me, tx, ty = lax.axis_index("freq"), lax.axis_index("tx"), lax.axis_index("ty")
    _, freqs, rows, cols = wave_hbm.shape
    steps = bins.shape[0]
    orders = table.shape[1]
    row_tiles, col_tiles = rows // 8, cols // LANES
    tiles = row_tiles * col_tiles
    chunks = min(n, tiles)
    per = tiles // chunks
    fields = 2 * freqs
    mine, group = lax.rem(me, chunks), lax.div(me, chunks) * chunks
    side = max(outs)
    side_tiles = side // 8
    wide = side_tiles > 0

    up, down = lax.rem(tx + n_tx - 1, n_tx), lax.rem(tx + 1, n_tx)
    left, right = lax.rem(ty + n_ty - 1, n_ty), lax.rem(ty + 1, n_ty)
    no_down = jnp.where(tx == n_tx - 1, 1, 0)
    no_up = jnp.where(tx == 0, 1, 0)
    no_right = jnp.where(ty == n_ty - 1, 1, 0)
    no_left = jnp.where(ty == 0, 1, 0)

    inputs = [
        pltpu.make_async_copy(slabs_hbm, slabs, in_sem.at[0]),
        pltpu.make_async_copy(wave_hbm, wv[0], in_sem.at[1]),
        pltpu.make_async_copy(bins_hbm, bins, in_sem.at[2]),
    ]
    for copy in inputs:
        copy.start()
    for e in range(2):
        lnd[e][...] = jnp.zeros_like(lnd[e])

    def there(x, y):
        return {"tx": x, "ty": y}

    def peer(d):
        return lax.rem(me + d, n)

    barrier = pltpu.get_barrier_semaphore()
    for d in range(1, n):
        pl.semaphore_signal(barrier, inc=1, device_id={"freq": peer(d)}, device_id_type=MESH)
    for x in (up, tx, down):
        for y in (left, ty, right):
            if x is not tx or y is not ty:
                pl.semaphore_signal(barrier, inc=1, device_id=there(x, y), device_id_type=MESH)

    def remote(src, dst, send, recv, to):
        return pltpu.make_async_remote_copy(
            src_ref=src, dst_ref=dst, send_sem=send, recv_sem=recv, device_id=to, device_id_type=MESH
        )

    def wait_for(ref, sem):
        pltpu.make_async_copy(ref, ref, sem).wait()

    def parts(g):
        if g in (0, 3):
            return src1.at[g // 3], land1.at[g // 3], dst1.at[g // 3]
        return src3.at[g - 1], land3.at[g - 1], dst3.at[g - 1]

    def chunk_at(ref, c):
        if per == 1:
            return ref.at[:, pl.ds(lax.div(c, col_tiles), 1), pl.ds(lax.rem(c, col_tiles), 1)]
        high = per // col_tiles
        return ref.at[:, pl.ds(c * high, high)]

    def scatter(g):
        src, land, _ = parts(g)
        for d in range(1, n):
            to = peer(d)
            remote(
                chunk_at(src, lax.rem(to, chunks)), land.at[d], rs_send.at[g], rs_recv.at[g], {"freq": to}
            ).start()

    def reduce_and_gather(g):
        src, land, dst = parts(g)
        wait_for(land.at[1:n], rs_recv.at[g])
        total = chunk_at(src, mine)[...]
        for d in range(1, n):
            total = total + land[d]
        here = chunk_at(dst, mine)
        here[...] = total
        for d in range(1, chunks):
            remote(here, here, ag_send.at[g], ag_recv.at[g], {"freq": group + lax.rem(mine + d, chunks)}).start()

    def gather_wait(g, sem):
        wait_for(parts(g)[1].at[1:chunks], sem.at[g])

    halo = [DEG + outs[0], DEG + outs[1]]

    def rows_up(e):
        w = halo[e]
        return remote(wv[e].at[:, :, 0:w], lnd[e].at[:, :, 0:w], halo_send.at[e, 0], halo_recv.at[e, 0], there(up, ty))

    def rows_down(e):
        w = halo[e]
        return remote(
            wv[e].at[:, :, rows - w : rows],
            lnd[e].at[:, :, w : 2 * w],
            halo_send.at[e, 1],
            halo_recv.at[e, 1],
            there(down, ty),
        )

    def columns(e):
        w = halo[e]
        copies = []
        for i, pk, landing, y in ((2, pk_l[e], in_r[e], left), (3, pk_r[e], in_l[e], right)):
            for src, dst, x in (
                (pk, landing.at[0:rows], tx),
                (pk.at[0:w], landing.at[rows : rows + w], up),
                (pk.at[rows - w : rows], landing.at[rows + w : rows + 2 * w], down),
            ):
                copies.append(remote(src, dst, halo_send.at[e, i], halo_recv.at[e, i], there(x, y)))
        return copies

    def send_halos(e):
        packed_l = packed_r = None
        lane = lax.broadcasted_iota(jnp.int32, (rows, LANES), 1)
        for i in range(fields):
            c, f = i // freqs, i % freqs
            start = wv[e][c, f, :, 0:LANES]
            end = wv[e][c, f, :, cols - LANES : cols]
            if i == 0:
                packed_l, packed_r = start, end
            else:
                packed_l = jnp.where(lane // GROUP == i, pltpu.roll(start, i * GROUP, 1), packed_l)
                packed_r = jnp.where(lane // GROUP == i - 1, pltpu.roll(end, i * GROUP, 1), packed_r)
        pk_l[e][...] = packed_l
        pk_r[e][...] = packed_r
        return lambda: start_halos(e)

    def start_halos(e):
        pl.when(tx > 0)(lambda: rows_up(e).start())
        pl.when(tx < n_tx - 1)(lambda: rows_down(e).start())
        for copy in columns(e):
            copy.start()

    def halo_recv_wait(e):
        pl.when(tx < n_tx - 1)(lambda: rows_up(e).wait_recv())
        pl.when(tx > 0)(lambda: rows_down(e).wait_recv())
        wait_for(in_r[e], halo_recv.at[e, 2])
        wait_for(in_l[e], halo_recv.at[e, 3])

    def halo_send_wait(e):
        pl.when(tx > 0)(lambda: rows_up(e).wait_send())
        pl.when(tx < n_tx - 1)(lambda: rows_down(e).wait_send())
        wait_for(in_r[e], halo_send.at[e, 2])
        wait_for(in_l[e], halo_send.at[e, 3])

    late = slice(1, steps - 1)

    def side_copies(g):
        if g == 0:
            pieces = [
                (0, bins.at[late, 0:side], bins_dn, up, ty),
                (1, bins.at[late, rows - side : rows], bins_up, down, ty),
            ]
            for i, landing, cs, y in (
                (2, bins_r, slice(0, LANES), left),
                (3, bins_l, slice(cols - LANES, cols), right),
            ):
                pieces += [
                    (i, bins.at[late, :, cs], landing.at[:, 0:rows], tx, y),
                    (i, bins.at[late, 0:side, cs], landing.at[:, rows : rows + side], up, y),
                    (i, bins.at[late, rows - side : rows, cs], landing.at[:, rows + side : rows + 2 * side], down, y),
                ]
        else:
            count, high = steps - 2, side_tiles
            src = dst3.at[0, 0:count]
            pieces = [
                (0, src.at[:, 0:high], frac_dn, up, ty),
                (1, src.at[:, row_tiles - high : row_tiles], frac_up, down, ty),
            ]
            for i, landing, ct, y in ((2, frac_r, 0, left), (3, frac_l, col_tiles - 1, right)):
                pieces += [
                    (i, src.at[:, :, ct], landing.at[:, 0:row_tiles], tx, y),
                    (i, src.at[:, 0:high, ct], landing.at[:, row_tiles : row_tiles + high], up, y),
                    (
                        i,
                        src.at[:, row_tiles - high : row_tiles, ct],
                        landing.at[:, row_tiles + high : row_tiles + 2 * high],
                        down,
                        y,
                    ),
                ]
        return [remote(a, b, side_send.at[g, i], side_recv.at[g, i], there(x, y)) for i, a, b, x, y in pieces]

    def side_wait(g, sem):
        for i, landing in enumerate(((bins_dn, bins_up, bins_r, bins_l), (frac_dn, frac_up, frac_r, frac_l))[g]):
            wait_for(landing, sem.at[g, i])

    def place(s, r):
        high = outs[s] // 8
        if r < row_tiles:
            return 0, r
        if r < row_tiles + high:
            return 1, r - row_tiles
        return 2, r - 2 * high

    def grid(s):
        high = outs[s] // 8
        return [
            (r, c) for r in range(row_tiles + 2 * high) for c in range(col_tiles + (1 if high else 0))
        ]

    lane8 = lax.broadcasted_iota(jnp.int32, (8, LANES), 1)

    def bins_tile(s, r, c):
        part, t = place(s, r)
        b = t - (row_tiles - side_tiles) if part == 2 else t
        if c < col_tiles:
            cs = slice(LANES * c, LANES * c + LANES)
            if part == 0:
                return bins[s, 8 * t : 8 * t + 8, cs]
            return (bins_dn, bins_up)[part - 1][s - 1, 8 * b : 8 * b + 8, cs]
        at = (0, rows, rows + side)[part] + 8 * b
        return jnp.where(lane8 < LANES // 2, bins_r[s - 1, at : at + 8], bins_l[s - 1, at : at + 8])

    def frac_tile(s, r, c):
        part, t = place(s, r)
        b = t - (row_tiles - side_tiles) if part == 2 else t
        if c < col_tiles:
            if part == 0:
                return dst1[0, 0, t, c] if s == 0 else dst3[0, s - 1, t, c]
            return (frac_dn, frac_up)[part - 1][s - 1, b, c]
        at = (0, row_tiles, row_tiles + side_tiles)[part] + b
        return jnp.where(lane8 < LANES // 2, frac_r[s - 1, at], frac_l[s - 1, at])

    inputs[0].wait()
    per_slab = slabs.shape[0]
    for j in range(steps):
        owner = owners[j]
        src = src1.at[0, 0] if j == 0 else src3.at[0, j - 1]
        for r in range(row_tiles):
            for c in range(col_tiles):
                value = jnp.zeros((8, LANES), jnp.float32)
                for i in range(per_slab):
                    tile = slabs[i, 8 * r : 8 * r + 8, LANES * c : LANES * c + LANES]
                    value = jnp.where(jnp.full((8, LANES), owner) == me * per_slab + i, tile, value)
                src[r, c] = value

    inputs[1].wait()
    send_halos(0)
    inputs[2].wait()
    pl.semaphore_wait(barrier, n - 1 + 8)
    scatter(0)
    start_halos(0)
    if wide:
        for copy in side_copies(0):
            copy.start()
    scatter(1)

    tab_a[...] = jnp.zeros_like(tab_a)
    for c in range(2):
        for f in range(freqs):
            tab_a[c * freqs + f, 0:orders, 0 : table.shape[3]] = table[c, :, f]
    for i in range(fields):
        tab_d[i] = pltpu.roll(tab_a[i], LANES - 1, 1) - tab_a[i]

    ext_cols = cols + LANES
    c = lax.broadcasted_iota(jnp.int32, (8, ext_cols), 1)
    beside = jnp.where(c >= cols + LANES // 2, no_left, jnp.where(c >= cols, no_right, 0))
    for i, no_row in enumerate((0, no_down, no_up)):
        mask[i] = jnp.where(beside + no_row > 0, 0.0, 0.25)

    def quarter(w):
        high = w // 8
        return jnp.concatenate([mask[0]] * row_tiles + [mask[1]] * high + [mask[2]] * high, axis=0)

    def lookup(s):
        def one(i, carry):
            for r, c in grid(s):
                rs, cs = slice(8 * r, 8 * r + 8), slice(LANES * c, LANES * c + LANES)
                index = bins_tile(s, r, c)
                for k in range(orders):
                    for tab, co in ((tab_a, co_a[s]), (tab_d, co_d[s])):
                        row = jnp.broadcast_to(tab[i, k : k + 1, :], (8, LANES))
                        co[i, k, rs, cs] = jnp.take_along_axis(row, index, axis=1, mode="promise_in_bounds")
            return carry

        lax.fori_loop(0, fields, one, 0)

    def unpack(e):
        w = halo[e]
        ext = rows + 2 * w
        lane = lax.broadcasted_iota(jnp.int32, (ext, LANES), 1)
        one_roll = 2 * w <= GROUP
        if one_roll:
            both = jnp.where(lax.rem(lane, GROUP) < GROUP // 2, in_r[e][...], in_l[e][...])
        for i in range(fields):
            by = (LANES - i * GROUP) % LANES
            turn = (lambda v: pltpu.roll(v, by, 1)) if by else (lambda v: v)
            if one_roll:
                beyond = turn(both)
            else:
                beyond = jnp.where(lane < LANES // 2, turn(in_r[e][...]), turn(in_l[e][...]))
            own = jnp.concatenate([wv[e][i // freqs, i % freqs], lnd[e][i // freqs, i % freqs]], axis=0)
            t = jnp.concatenate([own, beyond], axis=1)
            first[e][i] = jnp.where(quarter(w) > 0.0, t, 0.0)

    def recurrence(s):
        w = outs[s] + DEG
        ext = rows + 2 * w

        def term(k, i):
            return first[s][i] if k == 0 else tk[k - 1, i, 0:ext]

        for k in range(1, orders):
            twice, summed, moved = [], [], []
            for i in range(fields):
                t = term(k - 1, i)
                twice.append(t + t)
                summed.append(twice[i] + (pltpu.roll(t, 1, 0) + pltpu.roll(t, ext - 1, 0)))
            for i in range(fields):
                moved.append(pltpu.roll(summed[i], 1, 1) + pltpu.roll(summed[i], ext_cols - 1, 1))
            for i in range(fields):
                smooth = (summed[i] + summed[i] + moved[i]) * quarter(w)
                if k == 1:
                    tk[0, i, 0:ext] = 0.5 * (smooth - twice[i])
                else:
                    tk[k - 1, i, 0:ext] = (smooth - term(k - 2, i)) - twice[i]

    scale = 1.0 / math.sqrt(freqs * n)

    def combine(s):
        image = src1.at[1, 0] if s == steps - 1 else src3.at[1, s]
        for r, c in grid(s):
            rs, cs = slice(8 * r, 8 * r + 8), slice(LANES * c, LANES * c + LANES)
            part, t = place(s, r)
            at = 8 * r if part < 2 else 8 * r + 2 * DEG
            ts = slice(at, at + 8)
            fraction = frac_tile(s, r, c)
            summed = None
            for f in range(freqs):
                re = im = None
                for k in range(orders):
                    t_re = first[s][f, ts, cs] if k == 0 else tk[k - 1, f, ts, cs]
                    t_im = first[s][freqs + f, ts, cs] if k == 0 else tk[k - 1, freqs + f, ts, cs]
                    c_re = co_a[s][f, k, rs, cs] + fraction * co_d[s][f, k, rs, cs]
                    c_im = co_a[s][freqs + f, k, rs, cs] + fraction * co_d[s][freqs + f, k, rs, cs]
                    add_re = c_re * t_re - c_im * t_im
                    add_im = c_re * t_im + c_im * t_re
                    re = add_re if k == 0 else re + add_re
                    im = add_im if k == 0 else im + add_im
                if s == steps - 1:
                    wave_out[0, f, rs, cs] = re
                    wave_out[1, f, rs, cs] = im
                elif s == 0:
                    wv[1][0, f, rs, cs] = re
                    wv[1][1, f, rs, cs] = im
                else:
                    first[s + 1][f, rs, cs] = re
                    first[s + 1][freqs + f, rs, cs] = im
                summed = re if f == 0 else summed + re
            if part == 0 and c < col_tiles:
                image[t, c] = summed * scale

    lookup(0)
    reduce_and_gather(0)
    halo_recv_wait(0)
    unpack(0)
    recurrence(0)
    reduce_and_gather(1)
    gather_wait(0, ag_recv)
    combine(0)
    send_halos(1)
    start_halos(1)
    if wide:
        side_wait(0, side_recv)
    lookup(1)
    gather_wait(1, ag_recv)
    if wide:
        for copy in side_copies(1):
            copy.start()
    for s in range(2, steps):
        lookup(s)
    halo_recv_wait(1)
    unpack(1)
    for s in range(1, steps):
        recurrence(s)
        if s == 1 and wide:
            side_wait(1, side_recv)
        combine(s)
        if s == steps - 2:
            scatter(2)
    scatter(3)
    reduce_and_gather(2)
    reduce_and_gather(3)

    def put_image(j, src):
        for r in range(row_tiles):
            for c in range(col_tiles):
                images[j, 8 * r : 8 * r + 8, LANES * c : LANES * c + LANES] = src[r, c]

    gather_wait(2, ag_recv)
    for j in range(steps - 1):
        put_image(j, dst3.at[1, j])
    for e in range(2):
        halo_send_wait(e)
        if wide:
            side_wait(e, side_send)
    for g in range(4):
        wait_for(parts(g)[1].at[1:n], rs_send.at[g])
    for g in range(3):
        gather_wait(g, ag_send)
    gather_wait(3, ag_recv)
    put_image(steps - 1, dst1.at[1, 0])
    gather_wait(3, ag_send)


def solution(mesh):
    n, n_tx, n_ty = (mesh.shape[axis] for axis in ("freq", "tx", "ty"))

    def on_device(wavefield, coef_table, velocity_bins, slab_fracs, owners):
        _, freqs, rows, cols = wavefield.shape
        orders = coef_table.shape[2]
        steps = velocity_bins.shape[0]
        row_tiles, col_tiles = rows // 8, cols // LANES
        tiles = row_tiles * col_tiles
        per = tiles // min(n, tiles)
        chunk = (per // col_tiles, col_tiles) if per > 1 else (1, 1)
        outs = widths(steps)
        side = max(outs)
        fields = 2 * freqs
        ext_cols = cols + LANES
        f32, i32 = jnp.float32, jnp.int32
        vmem = pl.BlockSpec(memory_space=pltpu.VMEM)
        hbm = pl.BlockSpec(memory_space=pltpu.HBM)
        dma = pltpu.SemaphoreType.DMA
        tile = (8, LANES)

        def ext(s):
            return rows + 2 * (outs[s] + DEG)

        coefs = [
            pltpu.VMEM((fields, orders, rows + 2 * w, cols + (LANES if w else 0)), f32) for w in outs
        ]
        scratch = [pltpu.VMEM(velocity_bins.shape, i32), pltpu.VMEM(slab_fracs.shape, f32)]
        scratch += [pltpu.VMEM((2, freqs, rows, cols), f32) for e in range(2)]
        scratch += [pltpu.VMEM((2, freqs, ext(e) - rows, cols), f32) for e in range(2)]
        scratch += [pltpu.VMEM((rows, LANES), f32) for _ in range(4)]
        scratch += [pltpu.VMEM((ext(e), LANES), f32) for e in (0, 1, 0, 1)]
        scratch += [pltpu.VMEM((fields, ext(s), ext_cols), f32) for s in range(steps)]
        scratch += coefs + coefs
        scratch += [
            pltpu.VMEM((orders - 1, fields, max(map(ext, range(steps))), ext_cols), f32),
            pltpu.VMEM((3, 8, ext_cols), f32),
            pltpu.VMEM((fields, 16, LANES), f32),
            pltpu.VMEM((fields, 16, LANES), f32),
        ]
        late, high = steps - 2, side // 8
        scratch += [pltpu.VMEM((late, side, cols), i32) for _ in range(2)]
        scratch += [pltpu.VMEM((late, rows + 2 * side, LANES), i32) for _ in range(2)]
        scratch += [pltpu.VMEM((late, high, col_tiles) + tile, f32) for _ in range(2)]
        scratch += [pltpu.VMEM((late, row_tiles + 2 * high) + tile, f32) for _ in range(2)]
        for lead in ((), (n,), ()):
            shape = (chunk if lead else (row_tiles, col_tiles)) + tile
            scratch += [pltpu.VMEM((2,) + lead + (m,) + shape, f32) for m in (1, steps - 1)]
        scratch += [dma((3,)), dma((2, 4)), dma((2, 4)), dma((2, 4)), dma((2, 4))]
        scratch += [dma((4,)) for _ in range(4)]
        return pl.pallas_call(
            functools.partial(kernel, (n, n_tx, n_ty), outs),
            out_shape=(
                jax.ShapeDtypeStruct(wavefield.shape, f32),
                jax.ShapeDtypeStruct((steps, rows, cols), f32),
            ),
            in_specs=[pl.BlockSpec(memory_space=pltpu.SMEM), hbm, vmem, hbm, hbm],
            out_specs=(vmem, vmem),
            scratch_shapes=scratch,
            compiler_params=pltpu.CompilerParams(
                collective_id=0, has_side_effects=True, vmem_limit_bytes=60 * 1024 * 1024
            ),
        )(owners, wavefield, jnp.transpose(coef_table, (0, 2, 1, 3)), velocity_bins, slab_fracs)

    in_specs = (
        P(None, "freq", "tx", "ty"),
        P(None, "freq", None, None),
        P(None, "tx", "ty"),
        P("freq", "tx", "ty"),
        P(),
    )
    out_specs = (P(None, "freq", "tx", "ty"), P(None, "tx", "ty"))
    return jax.shard_map(on_device, mesh=mesh, in_specs=in_specs, out_specs=out_specs, check_vma=False)
```

time: 872 us -> 60.2 us (0.07)
  the two profiles are of different devices: /device:TPU:64 before, /device:TPU:1 now
where the time goes in v3:
time: 60.2 us; the launch traced here: 60 us
  Pallas kernels  57 us (95%)
  local copies, waits for them, and re-layouts  2.26 us (4%)
  between operations  0.65 us (1%)
    pallas_call x1, Pallas kernels, on_device(): pl.pallas_call(functools.partial(kernel, (n, n_tx, n_ty), outs), out_shap...  57 us
    unnamed x4, local copies, waits for them, and re-layouts  2.26 us

profile of v3, /device:TPU:1, one launch (start us, length us, event | category | flops | bytes accessed | tf_op | source)
XLA Modules:
  0.0 60.0 jit_solution(5972428687728041475)
XLA Ops:
  0.6 57.0 %shard_map.68 = (f32[2,2,32,256]{3,2,1,0:T(8,128)}, f32[4,32,256]{2,1,0:T(8,128)}) custom-call(s32[4]{0:T(128)} %refs_0_.1, f32[2,2,32,256]{3,2,1,0:T(8,128)} %refs_1_.1, f32[2,9,2,32]{3,2,1,0:T(2,128)} %bitcast.1, s32[4,32,256]{2,1,0:T(8,128)} %refs_3_.1, f32[2,32,256]{2,1,0:T(8,128)} %refs_4_.1), custom_call_target="tpu_custom_call" | custom-call | tf_op jit(solution)/shard_map/pallas_call | solution.py:498
  57.7 0.0 copy-start
  57.7 1.6 %copy.9 = f32[2,2,32,256]{3,2,1,0:T(8,128)} copy(f32[2,2,32,256]{3,2,1,0:T(8,128)} %get-tuple-element.4) | data formatting | bytes 262144
  59.3 0.0 copy-done
  59.3 0.7 %copy.10 = f32[4,32,256]{2,1,0:T(8,128)} copy(f32[4,32,256]{2,1,0:T(8,128)S(1)} %copy-done) | data formatting | bytes 262144
Async XLA Ops:
  57.7 1.6 %copy-start = (f32[4,32,256]{2,1,0:T(8,128)S(1)}, f32[4,32,256]{2,1,0:T(8,128)}, u32[]{:S(2)}) copy-start(f32[4,32,256]{2,1,0:T(8,128)} %get-tuple-element.5) | copy-start | bytes 393220

commit v4 on v3

--- a/solution.py
+++ b/solution.py
@@ -33,7 +33,7 @@
     first, co_a, co_d = (take(len(outs)) for _ in range(3))
     tk, mask, tab_a, tab_d = take(4)
     bins_dn, bins_up, bins_r, bins_l, frac_dn, frac_up, frac_r, frac_l = take(8)
-    src1, src3, land1, land3, dst1, dst3 = take(6)
+    src, land, dst = take(5), take(5), take(5)
     in_sem, halo_send, halo_recv, side_send, side_recv, rs_send, rs_recv, ag_send, ag_recv = take(9)
 
     me, tx, ty = lax.axis_index("freq"), lax.axis_index("tx"), lax.axis_index("ty")
@@ -89,11 +89,6 @@
     def wait_for(ref, sem):
         pltpu.make_async_copy(ref, ref, sem).wait()
 
-    def parts(g):
-        if g in (0, 3):
-            return src1.at[g // 3], land1.at[g // 3], dst1.at[g // 3]
-        return src3.at[g - 1], land3.at[g - 1], dst3.at[g - 1]
-
     def chunk_at(ref, c):
         if per == 1:
             return ref.at[:, pl.ds(lax.div(c, col_tiles), 1), pl.ds(lax.rem(c, col_tiles), 1)]
@@ -101,26 +96,24 @@
         return ref.at[:, pl.ds(c * high, high)]
 
     def scatter(g):
-        src, land, _ = parts(g)
         for d in range(1, n):
             to = peer(d)
             remote(
-                chunk_at(src, lax.rem(to, chunks)), land.at[d], rs_send.at[g], rs_recv.at[g], {"freq": to}
+                chunk_at(src[g], lax.rem(to, chunks)), land[g].at[d], rs_send.at[g], rs_recv.at[g], {"freq": to}
             ).start()
 
     def reduce_and_gather(g):
-        src, land, dst = parts(g)
-        wait_for(land.at[1:n], rs_recv.at[g])
-        total = chunk_at(src, mine)[...]
+        wait_for(land[g].at[1:n], rs_recv.at[g])
+        total = chunk_at(src[g], mine)[...]
         for d in range(1, n):
-            total = total + land[d]
-        here = chunk_at(dst, mine)
+            total = total + land[g][d]
+        here = chunk_at(dst[g], mine)
         here[...] = total
         for d in range(1, chunks):
             remote(here, here, ag_send.at[g], ag_recv.at[g], {"freq": group + lax.rem(mine + d, chunks)}).start()
 
     def gather_wait(g, sem):
-        wait_for(parts(g)[1].at[1:chunks], sem.at[g])
+        wait_for(land[g].at[1:chunks], sem.at[g])
 
     halo = [DEG + outs[0], DEG + outs[1]]
 
@@ -203,18 +196,18 @@
                 ]
         else:
             count, high = steps - 2, side_tiles
-            src = dst3.at[0, 0:count]
+            cut = dst[1].at[0:count]
             pieces = [
-                (0, src.at[:, 0:high], frac_dn, up, ty),
-                (1, src.at[:, row_tiles - high : row_tiles], frac_up, down, ty),
+                (0, cut.at[:, 0:high], frac_dn, up, ty),
+                (1, cut.at[:, row_tiles - high : row_tiles], frac_up, down, ty),
             ]
             for i, landing, ct, y in ((2, frac_r, 0, left), (3, frac_l, col_tiles - 1, right)):
                 pieces += [
-                    (i, src.at[:, :, ct], landing.at[:, 0:row_tiles], tx, y),
-                    (i, src.at[:, 0:high, ct], landing.at[:, row_tiles : row_tiles + high], up, y),
+                    (i, cut.at[:, :, ct], landing.at[:, 0:row_tiles], tx, y),
+                    (i, cut.at[:, 0:high, ct], landing.at[:, row_tiles : row_tiles + high], up, y),
                     (
                         i,
-                        src.at[:, row_tiles - high : row_tiles, ct],
+                        cut.at[:, row_tiles - high : row_tiles, ct],
                         landing.at[:, row_tiles + high : row_tiles + 2 * high],
                         down,
                         y,
@@ -258,7 +251,7 @@
         b = t - (row_tiles - side_tiles) if part == 2 else t
         if c < col_tiles:
             if part == 0:
-                return dst1[0, 0, t, c] if s == 0 else dst3[0, s - 1, t, c]
+                return dst[0][0, t, c] if s == 0 else dst[1][s - 1, t, c]
             return (frac_dn, frac_up)[part - 1][s - 1, b, c]
         at = (0, row_tiles, row_tiles + side_tiles)[part] + b
         return jnp.where(lane8 < LANES // 2, frac_r[s - 1, at], frac_l[s - 1, at])
@@ -267,14 +260,14 @@
     per_slab = slabs.shape[0]
     for j in range(steps):
         owner = owners[j]
-        src = src1.at[0, 0] if j == 0 else src3.at[0, j - 1]
+        chosen = src[0].at[0] if j == 0 else src[1].at[j - 1]
         for r in range(row_tiles):
             for c in range(col_tiles):
                 value = jnp.zeros((8, LANES), jnp.float32)
                 for i in range(per_slab):
                     tile = slabs[i, 8 * r : 8 * r + 8, LANES * c : LANES * c + LANES]
                     value = jnp.where(jnp.full((8, LANES), owner) == me * per_slab + i, tile, value)
-                src[r, c] = value
+                chosen[r, c] = value
 
     inputs[1].wait()
     send_halos(0)
@@ -285,7 +278,6 @@
     if wide:
         for copy in side_copies(0):
             copy.start()
-    scatter(1)
 
     tab_a[...] = jnp.zeros_like(tab_a)
     for c in range(2):
@@ -357,10 +349,14 @@
                 else:
                     tk[k - 1, i, 0:ext] = (smooth - term(k - 2, i)) - twice[i]
 
+    def image_at(s):
+        return (2, 0) if s == 0 else (4, 0) if s == steps - 1 else (3, s - 1)
+
     scale = 1.0 / math.sqrt(freqs * n)
 
     def combine(s):
-        image = src1.at[1, 0] if s == steps - 1 else src3.at[1, s]
+        g, j = image_at(s)
+        image = src[g].at[j]
         for r, c in grid(s):
             rs, cs = slice(8 * r, 8 * r + 8), slice(LANES * c, LANES * c + LANES)
             part, t = place(s, r)
@@ -393,24 +389,26 @@
                 image[t, c] = summed * scale
 
     lookup(0)
+    for s in range(steps - 1, 1, -1):
+        if s == steps - 2 and wide:
+            side_wait(0, side_recv)
+        lookup(s)
     reduce_and_gather(0)
+    scatter(1)
     halo_recv_wait(0)
     unpack(0)
     recurrence(0)
-    reduce_and_gather(1)
     gather_wait(0, ag_recv)
     combine(0)
     send_halos(1)
     start_halos(1)
-    if wide:
-        side_wait(0, side_recv)
+    reduce_and_gather(1)
     lookup(1)
     gather_wait(1, ag_recv)
     if wide:
         for copy in side_copies(1):
             copy.start()
-    for s in range(2, steps):
-        lookup(s)
+    scatter(2)
     halo_recv_wait(1)
     unpack(1)
     for s in range(1, steps):
@@ -419,30 +417,40 @@
             side_wait(1, side_recv)
         combine(s)
         if s == steps - 2:
-            scatter(2)
-    scatter(3)
-    reduce_and_gather(2)
-    reduce_and_gather(3)
-
-    def put_image(j, src):
+            scatter(3)
+    scatter(4)
+    for g in range(2, 5):
+        reduce_and_gather(g)
+
+    def put_image(s):
+        g, j = image_at(s)
         for r in range(row_tiles):
             for c in range(col_tiles):
-                images[j, 8 * r : 8 * r + 8, LANES * c : LANES * c + LANES] = src[r, c]
-
-    gather_wait(2, ag_recv)
-    for j in range(steps - 1):
-        put_image(j, dst3.at[1, j])
+                images[s, 8 * r : 8 * r + 8, LANES * c : LANES * c + LANES] = dst[g][j, r, c]
+
+    for g in range(2, 4):
+        gather_wait(g, ag_recv)
+    for s in range(steps - 1):
+        put_image(s)
     for e in range(2):
         halo_send_wait(e)
         if wide:
             side_wait(e, side_send)
+    for g in range(5):
+        wait_for(land[g].at[1:n], rs_send.at[g])
     for g in range(4):
-        wait_for(parts(g)[1].at[1:n], rs_send.at[g])
-    for g in range(3):
         gather_wait(g, ag_send)
-    gather_wait(3, ag_recv)
-    put_image(steps - 1, dst1.at[1, 0])
-    gather_wait(3, ag_send)
+    gather_wait(4, ag_recv)
+    put_image(steps - 1)
+    gather_wait(4, ag_send)
+
+
+def settle(wave, image, wave_out, images, sem):
+    copies = [pltpu.make_async_copy(wave, wave_out, sem.at[0]), pltpu.make_async_copy(image, images, sem.at[1])]
+    for copy in copies:
+        copy.start()
+    for copy in copies:
+        copy.wait()
 
 
 def solution(mesh):
@@ -492,10 +500,10 @@
         scratch += [pltpu.VMEM((late, row_tiles + 2 * high) + tile, f32) for _ in range(2)]
         for lead in ((), (n,), ()):
             shape = (chunk if lead else (row_tiles, col_tiles)) + tile
-            scratch += [pltpu.VMEM((2,) + lead + (m,) + shape, f32) for m in (1, steps - 1)]
+            scratch += [pltpu.VMEM(lead + (m,) + shape, f32) for m in (1, steps - 1, 1, steps - 2, 1)]
         scratch += [dma((3,)), dma((2, 4)), dma((2, 4)), dma((2, 4)), dma((2, 4))]
-        scratch += [dma((4,)) for _ in range(4)]
-        return pl.pallas_call(
+        scratch += [dma((5,)) for _ in range(4)]
+        results = pl.pallas_call(
             functools.partial(kernel, (n, n_tx, n_ty), outs),
             out_shape=(
                 jax.ShapeDtypeStruct(wavefield.shape, f32),
@@ -508,6 +516,14 @@
                 collective_id=0, has_side_effects=True, vmem_limit_bytes=60 * 1024 * 1024
             ),
         )(owners, wavefield, jnp.transpose(coef_table, (0, 2, 1, 3)), velocity_bins, slab_fracs)
+        return pl.pallas_call(
+            settle,
+            out_shape=tuple(jax.ShapeDtypeStruct(x.shape, f32) for x in results),
+            in_specs=[hbm, hbm],
+            out_specs=(hbm, hbm),
+            scratch_shapes=[dma((2,))],
+            compiler_params=pltpu.CompilerParams(vmem_limit_bytes=60 * 1024 * 1024),
+        )(*results)
 
     in_specs = (
         P(None, "freq", "tx", "ty"),

time: 60.2 us -> 70.9 us (1.18)
  Pallas kernels: 57 us -> 70.1 us
  local copies, waits for them, and re-layouts: 2.26 us -> 0 us
    pallas_call x0 -> x1, Pallas kernels: none -> 9.06 us  [on_device(): pl.pallas_call(settle, out_shape=tuple((jax.ShapeDtypeStruct(x.shape, f32...]
    pallas_call x1, Pallas kernels: 57 us -> 61 us  [on_device(): pl.pallas_call(functools.partial(kernel, (n, n_tx, n_ty), outs), out_shap...]
    unnamed x4 -> x0, local copies, waits for them, and re-layouts: 2.26 us -> none
where the time goes in v4:
time: 70.9 us; the launch traced here: 70.7 us
  Pallas kernels  70.1 us (99%)
    pallas_call x1, Pallas kernels, on_device(): pl.pallas_call(functools.partial(kernel, (n, n_tx, n_ty), outs), out_shap...  61 us
    pallas_call x1, Pallas kernels, on_device(): pl.pallas_call(settle, out_shape=tuple((jax.ShapeDtypeStruct(x.shape, f32...  9.06 us

profile of v4, /device:TPU:1, one launch (start us, length us, event | category | flops | bytes accessed | tf_op | source)
XLA Modules:
  0.0 70.7 jit_solution(6015483640913598605)
XLA Ops:
  0.6 61.0 %shard_map.68 = (f32[2,2,32,256]{3,2,1,0:T(8,128)}, f32[4,32,256]{2,1,0:T(8,128)}) custom-call(s32[4]{0:T(128)} %refs_0_.1, f32[2,2,32,256]{3,2,1,0:T(8,128)} %refs_1_.1, f32[2,9,2,32]{3,2,1,0:T(2,128)} %bitcast.1, s32[4,32,256]{2,1,0:T(8,128)} %refs_3_.1, f32[2,32,256]{2,1,0:T(8,128)} %refs_4_.1), custom_call_target="tpu_custom_call" | custom-call | tf_op jit(solution)/shard_map/pallas_call | solution.py:506
  61.7 9.1 %shard_map.69 = (f32[2,2,32,256]{3,2,1,0:T(8,128)}, f32[4,32,256]{2,1,0:T(8,128)}) custom-call(f32[2,2,32,256]{3,2,1,0:T(8,128)} %get-tuple-element.4.wave, f32[4,32,256]{2,1,0:T(8,128)} %get-tuple-element.5.image), custom_call_target="tpu_custom_call" | custom-call | tf_op jit(solution)/shard_map/pallas_call | solution.py:519

commit v5 on v4

--- a/solution.py
+++ b/solution.py
@@ -15,7 +15,7 @@
 
 
 def widths(steps):
-    return [0] + [DEG * (steps - 1 - s) for s in range(1, steps)]
+    return [0] * (steps - 2) + [DEG, 0]
 
 
 def kernel(sizes, outs, *refs):
@@ -27,9 +27,9 @@
         del refs[:count]
         return got
 
-    owners, wave_hbm, table, bins_hbm, slabs_hbm, wave_out, images = take(7)
-    bins, slabs = take(2)
-    wv, lnd, pk_l, pk_r, in_r, in_l = (take(2) for _ in range(6))
+    owners, wave_hbm, table_hbm, bins_hbm, slabs_hbm, wave_out, images = take(7)
+    table, bins, slabs = take(3)
+    wv, lnd, pk_l, pk_r, in_r, in_l = (take(len(outs) - 1) for _ in range(6))
     first, co_a, co_d = (take(len(outs)) for _ in range(3))
     tk, mask, tab_a, tab_d = take(4)
     bins_dn, bins_up, bins_r, bins_l, frac_dn, frac_up, frac_r, frac_l = take(8)
@@ -48,7 +48,6 @@
     mine, group = lax.rem(me, chunks), lax.div(me, chunks) * chunks
     side = max(outs)
     side_tiles = side // 8
-    wide = side_tiles > 0
 
     up, down = lax.rem(tx + n_tx - 1, n_tx), lax.rem(tx + 1, n_tx)
     left, right = lax.rem(ty + n_ty - 1, n_ty), lax.rem(ty + 1, n_ty)
@@ -61,10 +60,11 @@
         pltpu.make_async_copy(slabs_hbm, slabs, in_sem.at[0]),
         pltpu.make_async_copy(wave_hbm, wv[0], in_sem.at[1]),
         pltpu.make_async_copy(bins_hbm, bins, in_sem.at[2]),
+        pltpu.make_async_copy(table_hbm, table, in_sem.at[3]),
     ]
     for copy in inputs:
         copy.start()
-    for e in range(2):
+    for e in range(steps - 1):
         lnd[e][...] = jnp.zeros_like(lnd[e])
 
     def there(x, y):
@@ -115,7 +115,7 @@
     def gather_wait(g, sem):
         wait_for(land[g].at[1:chunks], sem.at[g])
 
-    halo = [DEG + outs[0], DEG + outs[1]]
+    halo = [DEG + w for w in outs[:-1]]
 
     def rows_up(e):
         w = halo[e]
@@ -177,26 +177,26 @@
         wait_for(in_r[e], halo_send.at[e, 2])
         wait_for(in_l[e], halo_send.at[e, 3])
 
-    late = slice(1, steps - 1)
+    late = steps - 2
 
     def side_copies(g):
         if g == 0:
             pieces = [
-                (0, bins.at[late, 0:side], bins_dn, up, ty),
-                (1, bins.at[late, rows - side : rows], bins_up, down, ty),
+                (0, bins.at[late : late + 1, 0:side], bins_dn, up, ty),
+                (1, bins.at[late : late + 1, rows - side : rows], bins_up, down, ty),
             ]
             for i, landing, cs, y in (
                 (2, bins_r, slice(0, LANES), left),
                 (3, bins_l, slice(cols - LANES, cols), right),
             ):
                 pieces += [
-                    (i, bins.at[late, :, cs], landing.at[:, 0:rows], tx, y),
-                    (i, bins.at[late, 0:side, cs], landing.at[:, rows : rows + side], up, y),
-                    (i, bins.at[late, rows - side : rows, cs], landing.at[:, rows + side : rows + 2 * side], down, y),
+                    (i, bins.at[late : late + 1, :, cs], landing.at[:, 0:rows], tx, y),
+                    (i, bins.at[late : late + 1, 0:side, cs], landing.at[:, rows : rows + side], up, y),
+                    (i, bins.at[late : late + 1, rows - side : rows, cs], landing.at[:, rows + side : rows + 2 * side], down, y),
                 ]
         else:
-            count, high = steps - 2, side_tiles
-            cut = dst[1].at[0:count]
+            high = side_tiles
+            cut = dst[1].at[late - 1 : late]
             pieces = [
                 (0, cut.at[:, 0:high], frac_dn, up, ty),
                 (1, cut.at[:, row_tiles - high : row_tiles], frac_up, down, ty),
@@ -242,9 +242,9 @@
             cs = slice(LANES * c, LANES * c + LANES)
             if part == 0:
                 return bins[s, 8 * t : 8 * t + 8, cs]
-            return (bins_dn, bins_up)[part - 1][s - 1, 8 * b : 8 * b + 8, cs]
+            return (bins_dn, bins_up)[part - 1][s - late, 8 * b : 8 * b + 8, cs]
         at = (0, rows, rows + side)[part] + 8 * b
-        return jnp.where(lane8 < LANES // 2, bins_r[s - 1, at : at + 8], bins_l[s - 1, at : at + 8])
+        return jnp.where(lane8 < LANES // 2, bins_r[s - late, at : at + 8], bins_l[s - late, at : at + 8])
 
     def frac_tile(s, r, c):
         part, t = place(s, r)
@@ -252,9 +252,9 @@
         if c < col_tiles:
             if part == 0:
                 return dst[0][0, t, c] if s == 0 else dst[1][s - 1, t, c]
-            return (frac_dn, frac_up)[part - 1][s - 1, b, c]
+            return (frac_dn, frac_up)[part - 1][s - late, b, c]
         at = (0, row_tiles, row_tiles + side_tiles)[part] + b
-        return jnp.where(lane8 < LANES // 2, frac_r[s - 1, at], frac_l[s - 1, at])
+        return jnp.where(lane8 < LANES // 2, frac_r[s - late, at], frac_l[s - late, at])
 
     inputs[0].wait()
     per_slab = slabs.shape[0]
@@ -275,10 +275,11 @@
     pl.semaphore_wait(barrier, n - 1 + 8)
     scatter(0)
     start_halos(0)
-    if wide:
-        for copy in side_copies(0):
-            copy.start()
-
+    scatter(1)
+    for copy in side_copies(0):
+        copy.start()
+
+    inputs[3].wait()
     tab_a[...] = jnp.zeros_like(tab_a)
     for c in range(2):
         for f in range(freqs):
@@ -350,7 +351,7 @@
                     tk[k - 1, i, 0:ext] = (smooth - term(k - 2, i)) - twice[i]
 
     def image_at(s):
-        return (2, 0) if s == 0 else (4, 0) if s == steps - 1 else (3, s - 1)
+        return (2, s) if s < late else (3 + s - late, 0)
 
     scale = 1.0 / math.sqrt(freqs * n)
 
@@ -378,9 +379,9 @@
                 if s == steps - 1:
                     wave_out[0, f, rs, cs] = re
                     wave_out[1, f, rs, cs] = im
-                elif s == 0:
-                    wv[1][0, f, rs, cs] = re
-                    wv[1][1, f, rs, cs] = im
+                elif s < late:
+                    wv[s + 1][0, f, rs, cs] = re
+                    wv[s + 1][1, f, rs, cs] = im
                 else:
                     first[s + 1][f, rs, cs] = re
                     first[s + 1][freqs + f, rs, cs] = im
@@ -389,34 +390,33 @@
                 image[t, c] = summed * scale
 
     lookup(0)
-    for s in range(steps - 1, 1, -1):
-        if s == steps - 2 and wide:
-            side_wait(0, side_recv)
-        lookup(s)
     reduce_and_gather(0)
-    scatter(1)
-    halo_recv_wait(0)
-    unpack(0)
-    recurrence(0)
-    gather_wait(0, ag_recv)
-    combine(0)
-    send_halos(1)
-    start_halos(1)
-    reduce_and_gather(1)
-    lookup(1)
-    gather_wait(1, ag_recv)
-    if wide:
-        for copy in side_copies(1):
-            copy.start()
-    scatter(2)
-    halo_recv_wait(1)
-    unpack(1)
-    for s in range(1, steps):
+    for s in range(steps):
+        if s <= late:
+            halo_recv_wait(s)
+            unpack(s)
         recurrence(s)
-        if s == 1 and wide:
+        if s < 2:
+            gather_wait(s, ag_recv)
+        if s == late:
             side_wait(1, side_recv)
         combine(s)
-        if s == steps - 2:
+        if s < late:
+            send_halos(s + 1)
+            start_halos(s + 1)
+        if s == 0:
+            reduce_and_gather(1)
+            lookup(1)
+            lookup(steps - 1)
+        elif s == 1:
+            for copy in side_copies(1):
+                copy.start()
+        if s == late - 1:
+            scatter(2)
+            side_wait(0, side_recv)
+        if 1 <= s < late:
+            lookup(s + 1)
+        if s == late:
             scatter(3)
     scatter(4)
     for g in range(2, 5):
@@ -432,10 +432,10 @@
         gather_wait(g, ag_recv)
     for s in range(steps - 1):
         put_image(s)
-    for e in range(2):
+    for e in range(steps - 1):
         halo_send_wait(e)
-        if wide:
-            side_wait(e, side_send)
+    for g in range(2):
+        side_wait(g, side_send)
     for g in range(5):
         wait_for(land[g].at[1:n], rs_send.at[g])
     for g in range(4):
@@ -443,14 +443,6 @@
     gather_wait(4, ag_recv)
     put_image(steps - 1)
     gather_wait(4, ag_send)
-
-
-def settle(wave, image, wave_out, images, sem):
-    copies = [pltpu.make_async_copy(wave, wave_out, sem.at[0]), pltpu.make_async_copy(image, images, sem.at[1])]
-    for copy in copies:
-        copy.start()
-    for copy in copies:
-        copy.wait()
 
 
 def solution(mesh):
@@ -480,11 +472,12 @@
         coefs = [
             pltpu.VMEM((fields, orders, rows + 2 * w, cols + (LANES if w else 0)), f32) for w in outs
         ]
-        scratch = [pltpu.VMEM(velocity_bins.shape, i32), pltpu.VMEM(slab_fracs.shape, f32)]
-        scratch += [pltpu.VMEM((2, freqs, rows, cols), f32) for e in range(2)]
-        scratch += [pltpu.VMEM((2, freqs, ext(e) - rows, cols), f32) for e in range(2)]
-        scratch += [pltpu.VMEM((rows, LANES), f32) for _ in range(4)]
-        scratch += [pltpu.VMEM((ext(e), LANES), f32) for e in (0, 1, 0, 1)]
+        scratch = [pltpu.VMEM((2, orders, freqs, coef_table.shape[3]), f32)]
+        scratch += [pltpu.VMEM(velocity_bins.shape, i32), pltpu.VMEM(slab_fracs.shape, f32)]
+        scratch += [pltpu.VMEM((2, freqs, rows, cols), f32) for e in range(steps - 1)]
+        scratch += [pltpu.VMEM((2, freqs, ext(e) - rows, cols), f32) for e in range(steps - 1)]
+        scratch += [pltpu.VMEM((rows, LANES), f32) for _ in range(2 * steps - 2)]
+        scratch += [pltpu.VMEM((ext(e), LANES), f32) for e in [*range(steps - 1)] * 2]
         scratch += [pltpu.VMEM((fields, ext(s), ext_cols), f32) for s in range(steps)]
         scratch += coefs + coefs
         scratch += [
@@ -493,37 +486,36 @@
             pltpu.VMEM((fields, 16, LANES), f32),
             pltpu.VMEM((fields, 16, LANES), f32),
         ]
-        late, high = steps - 2, side // 8
-        scratch += [pltpu.VMEM((late, side, cols), i32) for _ in range(2)]
-        scratch += [pltpu.VMEM((late, rows + 2 * side, LANES), i32) for _ in range(2)]
-        scratch += [pltpu.VMEM((late, high, col_tiles) + tile, f32) for _ in range(2)]
-        scratch += [pltpu.VMEM((late, row_tiles + 2 * high) + tile, f32) for _ in range(2)]
+        high = side // 8
+        scratch += [pltpu.VMEM((1, side, cols), i32) for _ in range(2)]
+        scratch += [pltpu.VMEM((1, rows + 2 * side, LANES), i32) for _ in range(2)]
+        scratch += [pltpu.VMEM((1, high, col_tiles) + tile, f32) for _ in range(2)]
+        scratch += [pltpu.VMEM((1, row_tiles + 2 * high) + tile, f32) for _ in range(2)]
         for lead in ((), (n,), ()):
             shape = (chunk if lead else (row_tiles, col_tiles)) + tile
-            scratch += [pltpu.VMEM(lead + (m,) + shape, f32) for m in (1, steps - 1, 1, steps - 2, 1)]
-        scratch += [dma((3,)), dma((2, 4)), dma((2, 4)), dma((2, 4)), dma((2, 4))]
+            scratch += [pltpu.VMEM(lead + (m,) + shape, f32) for m in (1, steps - 1, steps - 2, 1, 1)]
+        scratch += [dma((4,)), dma((steps - 1, 4)), dma((steps - 1, 4)), dma((2, 4)), dma((2, 4))]
         scratch += [dma((5,)) for _ in range(4)]
-        results = pl.pallas_call(
+        in_hbm = functools.partial(pltpu.with_memory_space_constraint, memory_space=pltpu.HBM)
+        return pl.pallas_call(
             functools.partial(kernel, (n, n_tx, n_ty), outs),
             out_shape=(
                 jax.ShapeDtypeStruct(wavefield.shape, f32),
                 jax.ShapeDtypeStruct((steps, rows, cols), f32),
             ),
-            in_specs=[pl.BlockSpec(memory_space=pltpu.SMEM), hbm, vmem, hbm, hbm],
+            in_specs=[pl.BlockSpec(memory_space=pltpu.SMEM), hbm, hbm, hbm, hbm],
             out_specs=(vmem, vmem),
             scratch_shapes=scratch,
             compiler_params=pltpu.CompilerParams(
-                collective_id=0, has_side_effects=True, vmem_limit_bytes=60 * 1024 * 1024
+                collective_id=0, has_side_effects=True, vmem_limit_bytes=40 * 1024 * 1024
             ),
-        )(owners, wavefield, jnp.transpose(coef_table, (0, 2, 1, 3)), velocity_bins, slab_fracs)
-        return pl.pallas_call(
-            settle,
-            out_shape=tuple(jax.ShapeDtypeStruct(x.shape, f32) for x in results),
-            in_specs=[hbm, hbm],
-            out_specs=(hbm, hbm),
-            scratch_shapes=[dma((2,))],
-            compiler_params=pltpu.CompilerParams(vmem_limit_bytes=60 * 1024 * 1024),
-        )(*results)
+        )(
+            owners,
+            in_hbm(wavefield),
+            in_hbm(jnp.transpose(coef_table, (0, 2, 1, 3))),
+            in_hbm(velocity_bins),
+            in_hbm(slab_fracs),
+        )
 
     in_specs = (
         P(None, "freq", "tx", "ty"),

time: 70.9 us -> 56.6 us (0.80)
  Pallas kernels: 70.1 us -> 53.9 us
  local copies, waits for them, and re-layouts: 0 us -> 1.96 us
    pallas_call x1 -> x0, Pallas kernels: 9.06 us -> none  [on_device(): pl.pallas_call(settle, out_shape=tuple((jax.ShapeDtypeStruct(x.shape, f32...]
    pallas_call x1, Pallas kernels: 61 us -> 53.9 us  [on_device(): pl.pallas_call(functools.partial(kernel, (n, n_tx, n_ty), outs), out_shap...]
    unnamed x0 -> x4, local copies, waits for them, and re-layouts: none -> 1.96 us
where the time goes in v5:
time: 56.6 us; the launch traced here: 56.5 us
  Pallas kernels  53.9 us (95%)
  local copies, waits for them, and re-layouts  1.96 us (3%)
  between operations  0.65 us (1%)
    pallas_call x1, Pallas kernels, on_device(): pl.pallas_call(functools.partial(kernel, (n, n_tx, n_ty), outs), out_shap...  53.9 us
    unnamed x4, local copies, waits for them, and re-layouts  1.96 us

profile of v5, /device:TPU:1, one launch (start us, length us, event | category | flops | bytes accessed | tf_op | source)
XLA Modules:
  0.0 56.5 jit_solution(4151484989420163123)
XLA Ops:
  0.6 0.0 copy-start
  0.6 0.6 %copy-done = s32[4]{0:T(128)S(1)} copy-done((s32[4]{0:T(128)S(1)}, s32[4]{0:T(128)}, u32[]{:S(2)}) %copy-start) | copy-done | bytes 40
  1.3 53.9 %shard_map.68 = (f32[2,2,32,256]{3,2,1,0:T(8,128)S(1)}, f32[4,32,256]{2,1,0:T(8,128)S(1)}) custom-call(s32[4]{0:T(128)S(1)} %copy-done, f32[2,2,32,256]{3,2,1,0:T(8,128)} %refs_1_.1, f32[2,9,2,32]{3,2,1,0:T(2,128)} %bitcast.1, s32[4,32,256]{2,1,0:T(8,128)} %refs_3_.1, f32[2,32,256]{2,1,0:T(8,128)} %refs_4_.1), custom_call_target="tpu_custom_call" | custom-call | tf_op jit(solution)/shard_map/pallas_call | solution.py:500
  55.2 0.7 %copy.9 = f32[2,2,32,256]{3,2,1,0:T(8,128)} copy(f32[2,2,32,256]{3,2,1,0:T(8,128)S(1)} %get-tuple-element.4) | data formatting | bytes 262144
  55.8 0.7 %copy.10 = f32[4,32,256]{2,1,0:T(8,128)} copy(f32[4,32,256]{2,1,0:T(8,128)S(1)} %get-tuple-element.5) | data formatting | bytes 262144
Async XLA Ops:
  0.6 0.7 %copy-start = (s32[4]{0:T(128)S(1)}, s32[4]{0:T(128)}, u32[]{:S(2)}) copy-start(s32[4]{0:T(128)} %refs_0_.1) | copy-start | bytes 52

commit v6 on v5

--- a/solution.py
+++ b/solution.py
@@ -56,6 +56,16 @@
     no_right = jnp.where(ty == n_ty - 1, 1, 0)
     no_left = jnp.where(ty == 0, 1, 0)
 
+    def there(x, y):
+        return {"tx": x, "ty": y}
+
+    def peer(d):
+        return lax.rem(me + d, n)
+
+    barrier = pltpu.get_barrier_semaphore()
+    for d in range(1, n):
+        pl.semaphore_signal(barrier, inc=1, device_id={"freq": peer(d)}, device_id_type=MESH)
+
     inputs = [
         pltpu.make_async_copy(slabs_hbm, slabs, in_sem.at[0]),
         pltpu.make_async_copy(wave_hbm, wv[0], in_sem.at[1]),
@@ -66,16 +76,6 @@
         copy.start()
     for e in range(steps - 1):
         lnd[e][...] = jnp.zeros_like(lnd[e])
-
-    def there(x, y):
-        return {"tx": x, "ty": y}
-
-    def peer(d):
-        return lax.rem(me + d, n)
-
-    barrier = pltpu.get_barrier_semaphore()
-    for d in range(1, n):
-        pl.semaphore_signal(barrier, inc=1, device_id={"freq": peer(d)}, device_id_type=MESH)
     for x in (up, tx, down):
         for y in (left, ty, right):
             if x is not tx or y is not ty:
@@ -348,7 +348,14 @@
                 if k == 1:
                     tk[0, i, 0:ext] = 0.5 * (smooth - twice[i])
                 else:
-                    tk[k - 1, i, 0:ext] = (smooth - term(k - 2, i)) - twice[i]
+                    t = (smooth - term(k - 2, i)) - twice[i]
+                    below = rows + outs[s]
+                    if k < orders - 1:
+                        tk[k - 1, i, 0:ext] = t
+                    else:
+                        tk[k - 1, i, 0:below] = t[0:below]
+                        if outs[s]:
+                            tk[k - 1, i, ext - outs[s] : ext] = t[ext - outs[s] : ext]
 
     def image_at(s):
         return (2, s) if s < late else (3 + s - late, 0)
@@ -510,7 +517,7 @@
                 collective_id=0, has_side_effects=True, vmem_limit_bytes=40 * 1024 * 1024
             ),
         )(
-            owners,
+            in_hbm(owners),
             in_hbm(wavefield),
             in_hbm(jnp.transpose(coef_table, (0, 2, 1, 3))),
             in_hbm(velocity_bins),

time: 56.6 us -> 55.9 us (0.988)
  local copies, waits for them, and re-layouts: 1.96 us -> 1.31 us
    unnamed x4 -> x2, local copies, waits for them, and re-layouts: 1.96 us -> 1.31 us
where the time goes in v6:
time: 55.9 us; the launch traced here: 55.8 us
  Pallas kernels  53.8 us (96%)
  local copies, waits for them, and re-layouts  1.31 us (2%)
  between operations  0.64 us (1%)
    pallas_call x1, Pallas kernels, on_device(): pl.pallas_call(functools.partial(kernel, (n, n_tx, n_ty), outs), out_shap...  53.8 us
    unnamed x2, local copies, waits for them, and re-layouts  1.31 us

profile of v6, /device:TPU:1, one launch (start us, length us, event | category | flops | bytes accessed | tf_op | source)
XLA Modules:
  0.0 55.8 jit_solution(3613309287797909134)
XLA Ops:
  0.6 53.8 %shard_map.68 = (f32[2,2,32,256]{3,2,1,0:T(8,128)S(1)}, f32[4,32,256]{2,1,0:T(8,128)S(1)}) custom-call(s32[4]{0:T(128)} %refs_0_.1, f32[2,2,32,256]{3,2,1,0:T(8,128)} %refs_1_.1, f32[2,9,2,32]{3,2,1,0:T(2,128)} %bitcast.1, s32[4,32,256]{2,1,0:T(8,128)} %refs_3_.1, f32[2,32,256]{2,1,0:T(8,128)} %refs_4_.1), custom_call_target="tpu_custom_call" | custom-call | tf_op jit(solution)/shard_map/pallas_call | solution.py:507
  54.4 0.7 %copy.9 = f32[2,2,32,256]{3,2,1,0:T(8,128)} copy(f32[2,2,32,256]{3,2,1,0:T(8,128)S(1)} %get-tuple-element.4) | data formatting | bytes 262144
  55.1 0.7 %copy.10 = f32[4,32,256]{2,1,0:T(8,128)} copy(f32[4,32,256]{2,1,0:T(8,128)S(1)} %get-tuple-element.5) | data formatting | bytes 262144
